TPU v7x, 256 devices: a whole 4x4x8 slice. The times are simulated.
256 devices in a mesh: slab: 16 (over y, z_lo), row: 2 (over core), col: 8 (over x, z_hi).
Axes of the slice: x: 4, y: 4, z: 8 (z_hi: 2, z_lo: 4; z = z_hi * 4 + z_lo), core: 2. Of those that a mesh axis runs over, the one named last changes fastest.
Arguments:
- pressure: float32 [64, 256, 1024], P('slab', 'row', 'col'), may hold values from -6 to 6
- velocity: float32 [3, 64, 256, 1024], P(None, 'slab', 'row', 'col'), may hold values from -6 to 6
- kappa: float32 [64, 256, 1024], P('slab', 'row', 'col'), may hold values from 0.5 to 2
- drive: float32 [64, 256, 1024], P('slab', 'row', 'col'), may hold values from -6 to 6
- adj_pressure_in: float32 [64, 256, 1024], P('slab', 'row', 'col'), may hold values from -6 to 6
- adj_velocity_in: float32 [3, 64, 256, 1024], P(None, 'slab', 'row', 'col'), may hold values from -6 to 6
- wall_mask: int32 [64, 256, 1024], P('slab', 'row', 'col'), may hold values 0 or 1
- wall_cells: int32 [16, 2, 8, 512], P('slab', 'row', 'col'), may hold values from 0 to 65535
- wall_rows: int32 [16, 2, 8, 512], P('slab', 'row', 'col'), may hold values from 0 to 2047
- slot_angle: float32 [16, 2, 8, 512], P('slab', 'row', 'col'), may hold values from 0 to 64
- wall_count: int32 [16, 2, 8], P('slab', 'row', 'col'), may hold values from 1 to 512, as said below
- step: int32 [1], replicated, may hold values from 0 to 4095
Outputs:
- adj_pressure: float32 [64, 256, 1024], P('slab', 'row', 'col')
- adj_velocity: float32 [3, 64, 256, 1024], P(None, 'slab', 'row', 'col')
- shape_grad: float32 [2048, 64], P(('slab', 'row', 'col'))
Inputs may be any that keep to these rules, and one draw needn't show every extreme that they name: `wall_count`: some device has all 512 slots live in every draw.
All inputs are finite; a program needn't handle non-finite values. No bound on the sum of `wall_mask` on one device may be relied on, other than what follows from the above.
Results may differ from a plain program's by a relative error of at most 0.00002.
Values sent between devices are 32-bit elements; how exact they have to be, the bound alone decides.
A program may use at most 64 MiB of HBM per device.

v0:
```python
import jax
import jax.numpy as jnp
from jax import lax
from jax.sharding import PartitionSpec as P

NROWS = 2048
ANG = 64


def padded_2(cells, sides, width):
    for axis, dim in sides:
        count = lax.axis_size(axis)
        ends = count - 1
        head = lax.slice_in_dim(cells, 0, width, axis=dim)
        tail = lax.slice_in_dim(cells, cells.shape[dim] - width, cells.shape[dim], axis=dim)
        cells = jnp.concatenate(
            [
                lax.ppermute(tail, axis, [(i, (i + 1) % count) for i in range(ends)]),
                cells,
                lax.ppermute(head, axis, [((i + 1) % count, i) for i in range(ends)]),
            ],
            axis=dim,
        )
    return cells


def crop_sides(field, axis, other, along):
    for dim in range(3):
        cut = along if dim == axis else other
        field = lax.slice_in_dim(field, cut, field.shape[dim] - cut, axis=dim)
    return field


def centered(padded, axis, width, extra):
    size = padded.shape[axis]
    upper = lax.slice_in_dim(padded, 2, size, axis=axis)
    lower = lax.slice_in_dim(padded, 0, size - 2, axis=axis)
    return crop_sides((upper - lower) * 0.5, axis, width, width - 1 - extra)


def spline_weights(angle):
    knots = jnp.arange(ANG, dtype=jnp.float32)
    dist = jnp.abs(angle[..., None] - knots)
    dist = jnp.minimum(dist, ANG - dist)
    outer = jnp.maximum(2.0 - dist, 0.0)
    inner = jnp.maximum(1.0 - dist, 0.0)
    return (outer * outer * outer - 4.0 * inner * inner * inner) / 6.0


def local(
    pressure,
    velocity,
    kappa,
    drive,
    adj_pressure_in,
    adj_velocity_in,
    wall_mask,
    wall_cells,
    wall_rows,
    slot_angle,
    wall_count,
    step,
):
    open_cells = 1.0 - wall_mask.astype(jnp.float32)
    phase = jnp.cos(0.5 * (step[0] % 97).astype(jnp.float32))
    scaled = kappa * adj_pressure_in
    padded = padded_2(jnp.stack([pressure, scaled]), (("slab", 1), ("row", 2), ("col", 3)), 1)
    slopes = [centered(padded[0], comp, 1, 0) for comp in range(3)]
    total = [adj_velocity_in[comp] + centered(padded[1], comp, 1, 0) for comp in range(3)]
    lam_u = [open_cells * total[comp] for comp in range(3)]
    padded_u = padded_2(jnp.stack(lam_u), (("slab", 1), ("row", 2), ("col", 3)), 1)
    divergence = (
        centered(padded_u[0], 0, 1, 0)
        + centered(padded_u[1], 1, 1, 0)
        + centered(padded_u[2], 2, 1, 0)
    )
    adj_pressure = adj_pressure_in + 0.3 * divergence
    moved = [velocity[comp] - 0.3 * slopes[comp] for comp in range(3)]
    moved[0] = moved[0] + drive * phase
    sens = -(total[0] * moved[0] + total[1] * moved[1] + total[2] * moved[2])
    cells = wall_cells.reshape(-1)
    values = sens.reshape(-1)[cells]
    live = jnp.arange(cells.shape[0], dtype=jnp.int32) < wall_count.reshape(-1)[0]
    values = jnp.where(live, values, 0.0)
    contrib = values[:, None] * spline_weights(slot_angle.reshape(-1))
    rows = wall_rows.reshape(-1)
    dense = jnp.zeros((NROWS, ANG), jnp.float32).at[rows].add(contrib)
    shape_grad = lax.psum_scatter(dense, ("slab", "row", "col"), scatter_dimension=0, tiled=True)
    return (adj_pressure, jnp.stack(lam_u), shape_grad)


def solution(mesh):
    in_specs = (
        P("slab", "row", "col"),
        P(None, "slab", "row", "col"),
        P("slab", "row", "col"),
        P("slab", "row", "col"),
        P("slab", "row", "col"),
        P(None, "slab", "row", "col"),
        P("slab", "row", "col"),
        P("slab", "row", "col", None),
        P("slab", "row", "col", None),
        P("slab", "row", "col", None),
        P("slab", "row", "col"),
        P(),
    )
    out_specs = (
        P("slab", "row", "col"),
        P(None, "slab", "row", "col"),
        P(("slab", "row", "col"), None),
    )
    return jax.shard_map(local, mesh=mesh, in_specs=in_specs, out_specs=out_specs, check_vma=False)
```

profile of v0, /device:TPU:1, one launch (start us, length us, event | category | flops | bytes accessed | tf_op | source)
XLA Modules:
  0.0 345.9 jit_solution(15520582255797227226)
XLA Ops:
  7.2 1.1 multiply_bitcast_fusion.3
  8.3 0.9 pad_maximum_fusion.6
  9.2 4.4 %collective-permute-start = (f32[2,1,128,128]{3,2,1,0:T(8,128)S(1)}, f32[2,1,128,128]{3,2,1,0:T(8,128)S(1)}, u32[]{:S(2)}, u32[]{:S(2)}) collective-permute-start(f32[2,1,128,128]{3,2,1,0:T(8,128)S(1)} %get-tuple-element.37), channel_id=1, source_target_pairs={{0,16},{16,32},{32,48},{48,64},{64,80},{80,96},{96,112},{112,128},... | collective-permute-start | bytes 393224 | tf_op jit(solution)/shard_map/ppermute | solution.py:18
  13.6 1.3 collective-permute-start.1
  14.9 0.7 compare_select_fusion
  15.7 7.3 %collective-permute-done.1 = f32[2,1,128,128]{3,2,1,0:T(8,128)S(1)} collective-permute-done((f32[2,1,128,128]{3,2,1,0:T(8,128)S(1)}, f32[2,1,128,128]{3,2,1,0:T(8,128)S(1)}, u32[]{:S(2)}, u32[]{:S(2)}) %collective-permute-start.1) | collective-permute-done | bytes 131104 | tf_op jit(solution)/shard_map/ppermute | solution.py:20
  23.1 1.3 collective-permute-start.2
  24.4 3.0 collective-permute-start.3
  27.4 0.8 collective-permute-done.3
  29.0 0.5 copy.47
  29.5 1.3 collective-permute-start.5
  30.8 9.0 %collective-permute-start.4 = (f32[2,6,130,1]{2,0,3,1:T(2,128)S(1)}, f32[2,6,130,1]{2,0,3,1:T(2,128)S(1)}, u32[]{:S(2)}, u32[]{:S(2)}) collective-permute-start(f32[2,6,130,1]{2,0,3,1:T(2,128)S(1)} %copy.46), channel_id=1, source_target_pairs={{0,1},{1,2},{2,3},{3,4},{4,5},{5,6},{6,7},{8,9},{9,10},{10,11},{11... | collective-permute-start | bytes 18728 | tf_op jit(solution)/shard_map/ppermute | solution.py:18
  42.0 0.8 pad_maximum_fusion.1
  43.6 0.8 copy-done.1
  44.9 2.7 collective-permute-start.6
  47.6 1.3 collective-permute-start.7
  48.9 0.5 fusion.13
  49.4 3.1 gather_fusion
  52.6 7.6 %collective-permute-done.7 = f32[3,1,128,128]{3,2,1,0:T(8,128)S(1)} collective-permute-done((f32[3,1,128,128]{3,2,1,0:T(8,128)S(1)}, f32[3,1,128,128]{3,2,1,0:T(8,128)S(1)}, u32[]{:S(2)}, u32[]{:S(2)}) %collective-permute-start.7) | collective-permute-done | bytes 196640 | tf_op jit(solution)/shard_map/ppermute | solution.py:20
  60.2 1.3 collective-permute-start.8
  61.5 3.0 collective-permute-start.9
  64.6 0.8 collective-permute-done.9
  65.9 0.9 copy.50
  66.8 0.9 copy.51
  67.7 1.3 collective-permute-start.11
  69.0 8.8 %collective-permute-start.10 = (f32[3,6,130,1]{2,1,3,0:T(8,128)S(1)}, f32[3,6,130,1]{2,1,3,0:T(8,128)S(1)}, u32[]{:S(2)}, u32[]{:S(2)}) collective-permute-start(f32[3,6,130,1]{2,1,3,0:T(8,128)S(1)} %copy.50), channel_id=1, source_target_pairs={{0,1},{1,2},{2,3},{3,4},{4,5},{5,6},{6,7},{8,9},{9,10},{10,11},{11... | collective-permute-start | bytes 28088 | tf_op jit(solution)/shard_map/ppermute | solution.py:18
  78.0 3.2 scatter_custom_fusion
  82.2 2.0 pad_maximum_fusion
  84.8 0.6 copy-done.6
  85.5 1.0 fusion.25
  86.4 251.3 %all-reduce.3.cloned.1.call-done = f32[2048,64]{1,0:T(8,128)} async-done(((f32[2048,64]{1,0:T(8,128)}), f32[2048,64]{1,0:T(8,128)}) %all-reduce.3.cloned.1.call-update) | async-done | bytes 524304
  337.8 1.3 constant_dynamic-slice_fusion
  (59 shorter events, 5.2 us)
Async XLA Ops:
  7.2 15.9 %copy-start = (f32[4,128,128]{2,1,0:T(8,128)S(1)}, f32[4,128,128]{2,1,0:T(8,128)}, u32[]{:S(2)}) copy-start(f32[4,128,128]{2,1,0:T(8,128)} %param.12) | copy-start | bytes 786436
  7.2 20.2 %copy-start.11 = (s32[1,1,1,512]{3,2,1,0:T(1,128)S(1)}, s32[1,1,1,512]{3,2,1,0:T(1,128)}, u32[]{:S(2)}) copy-start(s32[1,1,1,512]{3,2,1,0:T(1,128)} %param.20) | copy-start | bytes 6148
  7.2 330.6 %all-reduce.3.cloned.1.call-start = ((), (), s32[]{:S(2)}) async-start(), calls=%async_computation | async-start | bytes 2097152
  9.2 6.5 %collective-permute-start = (f32[2,1,128,128]{3,2,1,0:T(8,128)S(1)}, f32[2,1,128,128]{3,2,1,0:T(8,128)S(1)}, u32[]{:S(2)}, u32[]{:S(2)}) collective-permute-start(f32[2,1,128,128]{3,2,1,0:T(8,128)S(1)} %get-tuple-element.37), channel_id=1, source_target_pairs={{0,16},{16,32},{32,48},{48,64},{64,80},{80,96},{96,112},{112,128},... | collective-permute-start | bytes 393224 | tf_op jit(solution)/shard_map/ppermute | solution.py:18
  13.6 9.5 %collective-permute-start.1 = (f32[2,1,128,128]{3,2,1,0:T(8,128)S(1)}, f32[2,1,128,128]{3,2,1,0:T(8,128)S(1)}, u32[]{:S(2)}, u32[]{:S(2)}) collective-permute-start(f32[2,1,128,128]{3,2,1,0:T(8,128)S(1)} %get-tuple-element.38), channel_id=1, source_target_pairs={{16,0},{32,16},{48,32},{64,48},{80,64},{96,80},{112,96},{128,112},... | collective-permute-start | bytes 393224 | tf_op jit(solution)/shard_map/ppermute | solution.py:20
  23.1 4.4 %collective-permute-start.2 = (f32[2,6,1,128]{3,2,1,0:T(1,128)S(1)}, f32[2,6,1,128]{3,2,1,0:T(1,128)S(1)}, u32[]{:S(2)}, u32[]{:S(2)}) collective-permute-start(f32[2,6,1,128]{3,2,1,0:T(1,128)S(1)} %get-tuple-element.35), channel_id=1, source_target_pairs={{0,8},{1,9},{2,10},{3,11},{4,12},{5,13},{6,14},{7,15},{16,24},{17,... | collective-permute-start | bytes 18440 | tf_op jit(solution)/shard_map/ppermute | solution.py:18
  24.4 3.8 %collective-permute-start.3 = (f32[2,6,1,128]{3,2,1,0:T(1,128)S(1)}, f32[2,6,1,128]{3,2,1,0:T(1,128)S(1)}, u32[]{:S(2)}, u32[]{:S(2)}) collective-permute-start(f32[2,6,1,128]{3,2,1,0:T(1,128)S(1)} %get-tuple-element.36), channel_id=1, source_target_pairs={{8,0},{9,1},{10,2},{11,3},{12,4},{13,5},{14,6},{15,7},{24,16},{25,... | collective-permute-start | bytes 18440 | tf_op jit(solution)/shard_map/ppermute | solution.py:20
  29.5 12.1 %collective-permute-start.5 = (f32[2,6,130,1]{2,0,3,1:T(2,128)S(1)}, f32[2,6,130,1]{2,0,3,1:T(2,128)S(1)}, u32[]{:S(2)}, u32[]{:S(2)}) collective-permute-start(f32[2,6,130,1]{2,0,3,1:T(2,128)S(1)} %copy.47), channel_id=1, source_target_pairs={{1,0},{2,1},{3,2},{4,3},{5,4},{6,5},{7,6},{9,8},{10,9},{11,10},{12... | collective-permute-start | bytes 18728 | tf_op jit(solution)/shard_map/ppermute | solution.py:20
  30.8 10.4 %collective-permute-start.4 = (f32[2,6,130,1]{2,0,3,1:T(2,128)S(1)}, f32[2,6,130,1]{2,0,3,1:T(2,128)S(1)}, u32[]{:S(2)}, u32[]{:S(2)}) collective-permute-start(f32[2,6,130,1]{2,0,3,1:T(2,128)S(1)} %copy.46), channel_id=1, source_target_pairs={{0,1},{1,2},{2,3},{3,4},{4,5},{5,6},{6,7},{8,9},{9,10},{10,11},{11... | collective-permute-start | bytes 18728 | tf_op jit(solution)/shard_map/ppermute | solution.py:18
  43.3 1.1 copy-start.1
  43.3 1.2 copy-start.8
  44.8 4.1 %copy-start.7 = (f32[3,4,128,128]{3,2,1,0:T(8,128)S(1)}, f32[3,4,128,128]{3,2,1,0:T(8,128)}, u32[]{:S(2)}) copy-start(f32[3,4,128,128]{3,2,1,0:T(8,128)} %param.13) | copy-start | bytes 2359300
  44.8 4.1 %copy-start.9 = (f32[4,128,128]{2,1,0:T(8,128)S(1)}, f32[4,128,128]{2,1,0:T(8,128)}, u32[]{:S(2)}) copy-start(f32[4,128,128]{2,1,0:T(8,128)} %param.15) | copy-start | bytes 786436
  44.9 4.0 %copy-start.5 = (f32[3,4,128,128]{3,2,1,0:T(8,128)}, f32[3,4,128,128]{3,2,1,0:T(8,128)S(1)}, u32[]{:S(2)}) copy-start(f32[3,4,128,128]{3,2,1,0:T(8,128)S(1)} %pad_maximum_fusion.4) | copy-start | bytes 2359300
  44.9 7.7 %collective-permute-start.6 = (f32[3,1,128,128]{3,2,1,0:T(8,128)S(1)}, f32[3,1,128,128]{3,2,1,0:T(8,128)S(1)}, u32[]{:S(2)}, u32[]{:S(2)}) collective-permute-start(f32[3,1,128,128]{3,2,1,0:T(8,128)S(1)} %get-tuple-element.33), channel_id=1, source_target_pairs={{0,16},{16,32},{32,48},{48,64},{64,80},{80,96},{96,112},{112,128},... | collective-permute-start | bytes 589832 | tf_op jit(solution)/shard_map/ppermute | solution.py:18
  47.6 12.6 %collective-permute-start.7 = (f32[3,1,128,128]{3,2,1,0:T(8,128)S(1)}, f32[3,1,128,128]{3,2,1,0:T(8,128)S(1)}, u32[]{:S(2)}, u32[]{:S(2)}) collective-permute-start(f32[3,1,128,128]{3,2,1,0:T(8,128)S(1)} %get-tuple-element.34), channel_id=1, source_target_pairs={{16,0},{32,16},{48,32},{64,48},{80,64},{96,80},{112,96},{128,112},... | collective-permute-start | bytes 589832 | tf_op jit(solution)/shard_map/ppermute | solution.py:20
  52.6 12.8 %copy-start.2 = (f32[3,1,128,128]{3,2,1,0:T(8,128)}, f32[3,1,128,128]{3,2,1,0:T(8,128)S(1)}, u32[]{:S(2)}) copy-start(f32[3,1,128,128]{3,2,1,0:T(8,128)S(1)} %collective-permute-done.6) | copy-start | bytes 589828
  60.2 5.2 %copy-start.4 = (f32[3,1,128,128]{3,2,1,0:T(8,128)}, f32[3,1,128,128]{3,2,1,0:T(8,128)S(1)}, u32[]{:S(2)}) copy-start(f32[3,1,128,128]{3,2,1,0:T(8,128)S(1)} %collective-permute-done.7) | copy-start | bytes 589828
  60.2 4.4 %collective-permute-start.8 = (f32[3,6,1,128]{3,2,1,0:T(1,128)S(1)}, f32[3,6,1,128]{3,2,1,0:T(1,128)S(1)}, u32[]{:S(2)}, u32[]{:S(2)}) collective-permute-start(f32[3,6,1,128]{3,2,1,0:T(1,128)S(1)} %get-tuple-element.14), channel_id=1, source_target_pairs={{0,8},{1,9},{2,10},{3,11},{4,12},{5,13},{6,14},{7,15},{16,24},{17,... | collective-permute-start | bytes 27656 | tf_op jit(solution)/shard_map/ppermute | solution.py:18
  61.5 3.8 %collective-permute-start.9 = (f32[3,6,1,128]{3,2,1,0:T(1,128)S(1)}, f32[3,6,1,128]{3,2,1,0:T(1,128)S(1)}, u32[]{:S(2)}, u32[]{:S(2)}) collective-permute-start(f32[3,6,1,128]{3,2,1,0:T(1,128)S(1)} %get-tuple-element.15), channel_id=1, source_target_pairs={{8,0},{9,1},{10,2},{11,3},{12,4},{13,5},{14,6},{15,7},{24,16},{25,... | collective-permute-start | bytes 27656 | tf_op jit(solution)/shard_map/ppermute | solution.py:20
  65.9 11.9 %copy-start.10 = (f32[1,1,1,512]{3,2,1,0:T(1,128)S(1)}, f32[1,1,1,512]{3,2,1,0:T(1,128)}, u32[]{:S(2)}) copy-start(f32[1,1,1,512]{3,2,1,0:T(1,128)} %param.21) | copy-start | bytes 6148
  67.7 14.0 %collective-permute-start.11 = (f32[3,6,130,1]{2,1,3,0:T(8,128)S(1)}, f32[3,6,130,1]{2,1,3,0:T(8,128)S(1)}, u32[]{:S(2)}, u32[]{:S(2)}) collective-permute-start(f32[3,6,130,1]{2,1,3,0:T(8,128)S(1)} %copy.51), channel_id=1, source_target_pairs={{1,0},{2,1},{3,2},{4,3},{5,4},{6,5},{7,6},{9,8},{10,9},{11,10},{12... | collective-permute-start | bytes 28088 | tf_op jit(solution)/shard_map/ppermute | solution.py:20
  69.0 12.2 %collective-permute-start.10 = (f32[3,6,130,1]{2,1,3,0:T(8,128)S(1)}, f32[3,6,130,1]{2,1,3,0:T(8,128)S(1)}, u32[]{:S(2)}, u32[]{:S(2)}) collective-permute-start(f32[3,6,130,1]{2,1,3,0:T(8,128)S(1)} %copy.50), channel_id=1, source_target_pairs={{0,1},{1,2},{2,3},{3,4},{4,5},{5,6},{6,7},{8,9},{9,10},{10,11},{11... | collective-permute-start | bytes 28088 | tf_op jit(solution)/shard_map/ppermute | solution.py:18
  81.3 1.0 copy-start.3
  84.5 1.0 copy-start.6
Sparse Core Ops, SparseCore 0:
  81.4 256.3 all-reduce.2
where the time goes:
time: 347 us; the launch traced here: 346 us
  waiting for transfers between devices  268 us (77%)
  starting transfers between devices  38.7 us (11%)
  between operations  15.9 us (5%)
  local copies, waits for them, and re-layouts  12.3 us (4%)
  other arithmetic  11 us (3%)
    unnamed x2, waiting for transfers between devices  251 us
    ppermute x6, starting transfers between devices, padded_2(): lax.ppermute(tail, axis, [(i, (i + 1) % count) for i in range(ends)])  27.4 us
    ppermute x6, waiting for transfers between devices, padded_2(): lax.ppermute(head, axis, [((i + 1) % count, i) for i in range(ends)])  16.5 us
    ppermute x6, starting transfers between devices, padded_2(): lax.ppermute(head, axis, [((i + 1) % count, i) for i in range(ends)])  11.2 us
  transfers between devices with their start and end apart: 13, of which 6 were waited for; matrix products, arithmetic and copies ran while one was open for 4% of the time, Pallas kernels for 0%

commit v1 on v0

v1 whole, which is shorter than its diff:
```python
import functools

import jax
import jax.numpy as jnp
from jax import lax
from jax.experimental import pallas as pl
from jax.experimental.pallas import tpu as pltpu
from jax.sharding import PartitionSpec as P

ANG = 64
CX = 4
CY = 128
CZ = 128
WALL = 512
OWN = 8
MESH = pl.DeviceIdType.MESH
F32 = jnp.float32
BF16 = jnp.bfloat16


def pieces(value):
    high = value.astype(BF16)
    rest = value - high.astype(F32)
    mid = rest.astype(BF16)
    low = (rest - mid.astype(F32)).astype(BF16)
    return high, mid, low


def kernel(
    ns, nr, nc,
    p_in, v_in, kap_in, drv_in, ap_in, av_in, mask_in, cells_ref, rows_ref, angle_ref, count_ref, step_ref,
    ap_out, av_out, grad_out,
    pp, qq, kap, drv, ap, vel, avel, mask,
    lam0, lam1, lam2, apo,
    zsend, zrecv, lsend, lrecv,
    slots, vals, hot, weight, where_hot, sens_t, dense, parts,
    load_sem, store_sem, halo_send, halo_recv, lam_send, lam_recv,
    slot_send, slot_recv, val_send, val_recv, part_send, part_recv,
):
    nb = nr * nc
    s = lax.axis_index("slab")
    r = lax.axis_index("row")
    c = lax.axis_index("col")
    b = r * nc + c

    def slab_peer(k):
        return (lax.rem(s + k, ns), r, c)

    def block_peer(k):
        other = lax.rem(b + k, nb)
        return (s, lax.div(other, nc), lax.rem(other, nc))

    loads = [
        pltpu.make_async_copy(kap_in, kap, load_sem.at[0]),
        pltpu.make_async_copy(ap_in, ap, load_sem.at[1]),
        pltpu.make_async_copy(p_in, pp.at[pl.ds(1, CX), pl.ds(8, CY)], load_sem.at[2]),
        pltpu.make_async_copy(av_in, avel, load_sem.at[3]),
        pltpu.make_async_copy(mask_in, mask, load_sem.at[4]),
        pltpu.make_async_copy(v_in, vel, load_sem.at[5]),
        pltpu.make_async_copy(drv_in, drv, load_sem.at[6]),
    ]
    for copy in loads:
        copy.start()

    plane = jnp.zeros((CY, CZ), F32)
    for ref in (pp, qq):
        ref[0, pl.ds(8, CY)] = plane
        ref[CX + 1, pl.ds(8, CY)] = plane
        for x in range(CX):
            ref[x + 1, pl.ds(0, 8)] = jnp.zeros((8, CZ), F32)
            ref[x + 1, pl.ds(CY + 8, 8)] = jnp.zeros((8, CZ), F32)
    lam0[0] = plane
    lam0[CX + 1] = plane
    for x in range(CX):
        lam1[x, pl.ds(0, 8)] = jnp.zeros((8, CZ), F32)
        lam1[x, pl.ds(CY + 8, 8)] = jnp.zeros((8, CZ), F32)
    zrecv[...] = jnp.zeros_like(zrecv)
    lrecv[...] = jnp.zeros_like(lrecv)

    barrier = pltpu.get_barrier_semaphore()

    def greet_slab(k, _):
        pl.semaphore_signal(barrier, inc=1, device_id=slab_peer(k), device_id_type=MESH)
        return 0

    def greet_block(k, _):
        pl.semaphore_signal(barrier, inc=1, device_id=block_peer(k), device_id_type=MESH)
        return 0

    lax.fori_loop(1, ns, greet_slab, 0)
    lax.fori_loop(1, nb, greet_block, 0)

    lane = lax.broadcasted_iota(jnp.int32, (1, WALL), 1)
    own_rows = rows_ref[0, 0]
    live = lane < count_ref[0, 0, 0]
    slots[ns - 1, 0:1] = jnp.where(live, own_rows.astype(F32), -1.0)
    slots[ns - 1, 1:2] = angle_ref[0, 0]

    pl.semaphore_wait(barrier, ns - 1 + nb - 1)

    def slot_copy(k):
        return pltpu.make_async_remote_copy(
            src_ref=slots.at[ns - 1], dst_ref=slots.at[k - 1],
            send_sem=slot_send, recv_sem=slot_recv,
            device_id=slab_peer(k), device_id_type=MESH,
        )

    def send_slots(k, _):
        slot_copy(k).start()
        return 0

    def halo(src, dst, sem_at, send_sem, recv_sem, device):
        return pltpu.make_async_remote_copy(
            src_ref=src, dst_ref=dst, send_sem=send_sem.at[sem_at], recv_sem=recv_sem.at[sem_at],
            device_id=device, device_id_type=MESH,
        )

    rows_of = pl.ds(8, CY)
    s_up, s_down = jnp.minimum(s + 1, ns - 1), jnp.maximum(s - 1, 0)
    r_up, r_down = jnp.minimum(r + 1, nr - 1), jnp.maximum(r - 1, 0)
    c_up, c_down = jnp.minimum(c + 1, nc - 1), jnp.maximum(c - 1, 0)
    has = {
        "xu": s < ns - 1, "xd": s > 0, "yu": r < nr - 1, "yd": r > 0, "zu": c < nc - 1, "zd": c > 0,
    }

    def field_x(ref, base):
        return {
            "xu": halo(ref.at[CX, rows_of], ref.at[0, rows_of], base, halo_send, halo_recv, (s_up, r, c)),
            "xd": halo(ref.at[1, rows_of], ref.at[CX + 1, rows_of], base + 1, halo_send, halo_recv, (s_down, r, c)),
        }

    def field_y(ref, base):
        inner = pl.ds(1, CX)
        return {
            "yu": halo(ref.at[inner, pl.ds(CY, 8)], ref.at[inner, pl.ds(0, 8)], base, halo_send, halo_recv, (s, r_up, c)),
            "yd": halo(ref.at[inner, pl.ds(8, 8)], ref.at[inner, pl.ds(CY + 8, 8)], base + 1, halo_send, halo_recv, (s, r_down, c)),
        }

    q_x = field_x(qq, 0)
    p_x = field_x(pp, 2)
    q_y = field_y(qq, 4)
    p_y = field_y(pp, 6)
    pq_z = {
        "zu": halo(zsend.at[pl.ds(8, 8)], zrecv.at[pl.ds(0, 8)], 8, halo_send, halo_recv, (s, r, c_up)),
        "zd": halo(zsend.at[pl.ds(0, 8)], zrecv.at[pl.ds(8, 8)], 9, halo_send, halo_recv, (s, r, c_down)),
    }
    inner = pl.ds(0, CX)
    lam_x = {
        "xu": halo(lam0.at[CX], lam0.at[0], 0, lam_send, lam_recv, (s_up, r, c)),
        "xd": halo(lam0.at[1], lam0.at[CX + 1], 1, lam_send, lam_recv, (s_down, r, c)),
    }
    lam_y = {
        "yu": halo(lam1.at[inner, pl.ds(CY, 8)], lam1.at[inner, pl.ds(0, 8)], 2, lam_send, lam_recv, (s, r_up, c)),
        "yd": halo(lam1.at[inner, pl.ds(8, 8)], lam1.at[inner, pl.ds(CY + 8, 8)], 3, lam_send, lam_recv, (s, r_down, c)),
    }
    lam_z = {
        "zu": halo(lsend.at[pl.ds(8, 8)], lrecv.at[pl.ds(0, 8)], 4, lam_send, lam_recv, (s, r, c_up)),
        "zd": halo(lsend.at[pl.ds(0, 8)], lrecv.at[pl.ds(8, 8)], 5, lam_send, lam_recv, (s, r, c_down)),
    }

    def start(group):
        for side, copy in group.items():
            pl.when(has[side])(copy.start)

    opposite = {"xu": "xd", "xd": "xu", "yu": "yd", "yd": "yu", "zu": "zd", "zd": "zu"}

    def arrive(group):
        for side, copy in group.items():
            pl.when(has[opposite[side]])(copy.wait_recv)

    def sent(group):
        for side, copy in group.items():
            pl.when(has[side])(copy.wait_send)

    lax.fori_loop(1, ns, send_slots, 0)

    loads[0].wait()
    loads[1].wait()
    for x in (0, CX - 1):
        qq[x + 1, rows_of] = kap[x] * ap[x]
    start(q_x)
    for x in range(1, CX - 1):
        qq[x + 1, rows_of] = kap[x] * ap[x]
    start(q_y)
    loads[2].wait()
    start(p_x)
    start(p_y)
    for ref, at in ((pp, 0), (qq, CX)):
        for x in range(CX):
            turned = ref[x + 1, rows_of].T
            zsend[at + x:at + x + 1] = turned[0:1]
            zsend[8 + at + x:8 + at + x + 1] = turned[CZ - 1:CZ]
    start(pq_z)

    own_cells = cells_ref[0, 0]
    own_xy = own_cells >> 7
    own_z = own_cells & (CZ - 1)
    xy = lax.broadcasted_iota(jnp.int32, (CY, WALL), 0)
    for x in range(CX):
        where_hot[x * CY:(x + 1) * CY] = jnp.where(xy + x * CY == own_xy, 1.0, 0.0).astype(BF16)

    pltpu.make_async_copy(slots.at[pl.ds(0, ns - 1)], slots.at[pl.ds(0, ns - 1)], slot_recv).wait()
    width = nb * OWN
    first = (s * width).astype(F32)
    row_at = lax.broadcasted_iota(jnp.int32, (width, WALL), 0).astype(F32) + first
    knots = lax.broadcasted_iota(jnp.int32, (ANG, WALL), 0).astype(F32)

    def prepare(g, _):
        hot[g] = jnp.where(slots[g, 0:1] == row_at, 1.0, 0.0).astype(BF16)
        dist = jnp.abs(slots[g, 1:2] - knots)
        dist = jnp.minimum(dist, ANG - dist)
        outer = jnp.maximum(2.0 - dist, 0.0)
        near = jnp.maximum(1.0 - dist, 0.0)
        weight[g] = (outer * outer * outer - 4.0 * near * near * near) * (1.0 / 6.0)
        return 0

    lax.fori_loop(0, ns, prepare, 0)

    phase = jnp.cos(0.5 * jnp.full((1, CZ), lax.rem(step_ref[0], 97).astype(F32), F32))
    for copy in loads[3:]:
        copy.wait()
    for group in (q_x, q_y, p_x, p_y, pq_z):
        arrive(group)
    edge_t = jnp.concatenate([zrecv[...], jnp.zeros((CZ - 16, CZ), F32)], axis=0).T
    at_z = lax.broadcasted_iota(jnp.int32, (CY, CZ), 1)

    def along_z(field, low, high):
        upper = jnp.where(at_z == CZ - 1, high, pltpu.roll(field, CZ - 1, 1))
        lower = jnp.where(at_z == 0, low, pltpu.roll(field, 1, 1))
        return (upper - lower) * 0.5

    def slopes(ref, x, at):
        mid = ref[x + 1, rows_of]
        return (
            (ref[x + 2, rows_of] - ref[x, rows_of]) * 0.5,
            (ref[x + 1, pl.ds(9, CY)] - ref[x + 1, pl.ds(7, CY)]) * 0.5,
            along_z(mid, edge_t[:, at + x:at + x + 1], edge_t[:, 8 + at + x:8 + at + x + 1]),
        )

    for x in range(CX):
        dp = slopes(pp, x, 0)
        dq = slopes(qq, x, CX)
        free = 1.0 - mask[x].astype(F32)
        total = [avel[k, x] + dq[k] for k in range(3)]
        lam0[x + 1] = free * total[0]
        lam1[x, rows_of] = free * total[1]
        lam2[x] = free * total[2]
        sens = -(
            total[0] * (vel[0, x] - 0.3 * dp[0] + drv[x] * phase)
            + total[1] * (vel[1, x] - 0.3 * dp[1])
            + total[2] * (vel[2, x] - 0.3 * dp[2])
        )
        for i, piece in enumerate(pieces(sens.T)):
            sens_t[i * CZ:(i + 1) * CZ, x * CY:(x + 1) * CY] = piece

    picked = jnp.dot(sens_t[...], where_hot[...], preferred_element_type=F32)
    picked = picked[0:CZ] + picked[CZ:2 * CZ] + picked[2 * CZ:3 * CZ]
    z_at = lax.broadcasted_iota(jnp.int32, (CZ, WALL), 0)
    vals[ns - 1] = jnp.sum(jnp.where(z_at == own_z, picked, 0.0), axis=0, keepdims=True)

    def send_vals(k, _):
        pltpu.make_async_remote_copy(
            src_ref=vals.at[ns - 1], dst_ref=vals.at[k - 1], send_sem=val_send, recv_sem=val_recv,
            device_id=slab_peer(k), device_id_type=MESH,
        ).start()
        return 0

    lax.fori_loop(1, ns, send_vals, 0)

    start(lam_x)
    start(lam_y)
    for x in range(CX):
        turned = lam2[x].T
        lsend[x:x + 1] = turned[0:1]
        lsend[8 + x:9 + x] = turned[CZ - 1:CZ]
    start(lam_z)
    stores = [
        pltpu.make_async_copy(lam0.at[pl.ds(1, CX)], av_out.at[0], store_sem.at[0]),
        pltpu.make_async_copy(lam1.at[pl.ds(0, CX), rows_of], av_out.at[1], store_sem.at[1]),
        pltpu.make_async_copy(lam2, av_out.at[2], store_sem.at[2]),
    ]
    for copy in stores:
        copy.start()

    pltpu.make_async_copy(vals.at[pl.ds(0, ns - 1)], vals.at[pl.ds(0, ns - 1)], val_recv).wait()

    def add_up(g, total):
        scaled = jnp.concatenate(pieces(weight[g] * vals[g]), axis=0)
        return total + lax.dot_general(
            hot[g], scaled, (((1,), (1,)), ((), ())), preferred_element_type=F32
        )

    summed = lax.fori_loop(0, ns, add_up, jnp.zeros((width, 3 * ANG), F32))
    summed = summed[:, 0:ANG] + summed[:, ANG:2 * ANG] + summed[:, 2 * ANG:3 * ANG]
    dense[...] = jnp.concatenate([summed, jnp.zeros_like(summed)], axis=1).reshape(nb, OWN, 2 * ANG)

    def send_part(k, _):
        other = lax.rem(b + k, nb)
        pltpu.make_async_remote_copy(
            src_ref=dense.at[other], dst_ref=parts.at[k - 1], send_sem=part_send, recv_sem=part_recv,
            device_id=block_peer(k), device_id_type=MESH,
        ).start()
        return 0

    lax.fori_loop(1, nb, send_part, 0)

    for group in (lam_x, lam_y, lam_z):
        arrive(group)
    edge_l = jnp.concatenate([lrecv[...], jnp.zeros((CZ - 16, CZ), F32)], axis=0).T
    for x in range(CX):
        div = (
            (lam0[x + 2] - lam0[x]) * 0.5
            + (lam1[x, pl.ds(9, CY)] - lam1[x, pl.ds(7, CY)]) * 0.5
            + along_z(lam2[x], edge_l[:, x:x + 1], edge_l[:, 8 + x:9 + x])
        )
        apo[x] = ap[x] + 0.3 * div
    last = pltpu.make_async_copy(apo, ap_out, store_sem.at[3])
    last.start()

    pltpu.make_async_copy(parts, parts, part_recv).wait()
    grad_out[...] = (dense[b] + jnp.sum(parts[...], axis=0))[:, 0:ANG]

    for group in (q_x, q_y, p_x, p_y, pq_z, lam_x, lam_y, lam_z):
        sent(group)
    pltpu.make_async_copy(slots.at[pl.ds(0, ns - 1)], slots.at[pl.ds(0, ns - 1)], slot_send).wait()
    pltpu.make_async_copy(vals.at[pl.ds(0, ns - 1)], vals.at[pl.ds(0, ns - 1)], val_send).wait()
    pltpu.make_async_copy(parts, parts, part_send).wait()
    for copy in stores + [last]:
        copy.wait()


def local(ns, nr, nc, *args):
    nb = nr * nc
    anyspace = pl.BlockSpec(memory_space=pl.ANY)
    vmem = pl.BlockSpec(memory_space=pltpu.VMEM)
    smem = pl.BlockSpec(memory_space=pltpu.SMEM)
    block = (CX, CY, CZ)
    dma = pltpu.SemaphoreType.DMA
    return pl.pallas_call(
        functools.partial(kernel, ns, nr, nc),
        out_shape=(
            jax.ShapeDtypeStruct(block, F32),
            jax.ShapeDtypeStruct((3,) + block, F32),
            jax.ShapeDtypeStruct((OWN, ANG), F32),
        ),
        in_specs=[anyspace] * 7 + [vmem] * 3 + [smem] * 2,
        out_specs=(anyspace, anyspace, vmem),
        scratch_shapes=[
            pltpu.VMEM((CX + 2, CY + 16, CZ), F32),
            pltpu.VMEM((CX + 2, CY + 16, CZ), F32),
            pltpu.VMEM(block, F32),
            pltpu.VMEM(block, F32),
            pltpu.VMEM(block, F32),
            pltpu.VMEM((3,) + block, F32),
            pltpu.VMEM((3,) + block, F32),
            pltpu.VMEM(block, jnp.int32),
            pltpu.VMEM((CX + 2, CY, CZ), F32),
            pltpu.VMEM((CX, CY + 16, CZ), F32),
            pltpu.VMEM(block, F32),
            pltpu.VMEM(block, F32),
            pltpu.VMEM((16, CY), F32),
            pltpu.VMEM((16, CY), F32),
            pltpu.VMEM((16, CY), F32),
            pltpu.VMEM((16, CY), F32),
            pltpu.VMEM((ns, 2, WALL), F32),
            pltpu.VMEM((ns, 1, WALL), F32),
            pltpu.VMEM((ns, nb * OWN, WALL), BF16),
            pltpu.VMEM((ns, ANG, WALL), F32),
            pltpu.VMEM((CX * CY, WALL), BF16),
            pltpu.VMEM((3 * CZ, CX * CY), BF16),
            pltpu.VMEM((nb, OWN, 2 * ANG), F32),
            pltpu.VMEM((nb - 1, OWN, 2 * ANG), F32),
            dma((7,)), dma((4,)), dma((10,)), dma((10,)), dma((6,)), dma((6,)),
            dma, dma, dma, dma, dma, dma,
        ],
        compiler_params=pltpu.CompilerParams(
            collective_id=0, has_side_effects=True, vmem_limit_bytes=48 * 1024 * 1024
        ),
        cost_estimate=pl.CostEstimate(flops=10**9, bytes_accessed=4 * 10**6, transcendentals=0),
    )(*args)


def solution(mesh):
    names = ("slab", "row", "col")
    sizes = tuple(mesh.shape[name] for name in names)
    cells = P(*names)
    vector = P(None, *names)
    slot = P(*names, None)
    in_specs = (cells, vector, cells, cells, cells, vector, cells, slot, slot, slot, cells, P())
    out_specs = (cells, vector, P(names, None))
    return jax.shard_map(
        functools.partial(local, *sizes), mesh=mesh, in_specs=in_specs, out_specs=out_specs, check_vma=False
    )
```

time: 347 us -> 52.5 us (0.15)
  waiting for transfers between devices: 268 us -> 0 us
  Pallas kernels: 0 us -> 39.6 us
  starting transfers between devices: 38.7 us -> 0 us
  between operations: 15.9 us -> 1.98 us
  other arithmetic: 11 us -> 0 us
    unnamed x2 -> x0, waiting for transfers between devices: 251 us -> none
    pallas_call x0 -> x1, Pallas kernels: none -> 39.6 us  [local(): pl.pallas_call(functools.partial(kernel, ns, nr, nc), out_shape=(jax.Shap...]
    ppermute x12 -> x0, starting transfers between devices: 38.6 us -> none  [the longest x6 27.4 us: padded_2(): lax.ppermute(tail, axis, [(i, (i + 1) % count) for i in range(ends)])]
    ppermute x12 -> x0, waiting for transfers between devices: 16.7 us -> none  [the longest x6 16.5 us: padded_2(): lax.ppermute(head, axis, [((i + 1) % count, i) for i in range(ends)])]
    unnamed x25 -> x23, local copies, waits for them, and re-layouts: 2.78 us -> 10.5 us
    slice x11 -> x0, local copies, waits for them, and re-layouts: 4.38 us -> none  [the longest x5 2.08 us: padded_2(): lax.slice_in_dim(cells, cells.shape[dim] - width, cells.shape[dim], axis=...]
  transfers between devices with their start and end apart: 13 -> 0, of which waited for: 6 -> 0; matrix products, arithmetic and copies ran while one was open for 4% -> 0% of each run, Pallas kernels for 0% -> 0%
where the time goes in v1:
time: 52.5 us; the launch traced here: 52.1 us
  Pallas kernels  39.6 us (75%)
  local copies, waits for them, and re-layouts  10.5 us (20%)
  between operations  1.98 us (4%)
    pallas_call x1, Pallas kernels, local(): pl.pallas_call(functools.partial(kernel, ns, nr, nc), out_shape=(jax.Shap...  39.6 us
    unnamed x23, local copies, waits for them, and re-layouts  10.5 us

profile of v1, /device:TPU:1, one launch (start us, length us, event | category | flops | bytes accessed | tf_op | source)
XLA Modules:
  0.0 52.1 jit_solution(3954376658414269000)
XLA Ops:
  0.6 0.0 copy-start.7
  1.9 0.0 copy-done.7
  2.0 0.0 copy-start
  2.0 1.1 %copy-done = f32[3,4,128,128]{3,2,1,0:T(8,128)S(1)} copy-done((f32[3,4,128,128]{3,2,1,0:T(8,128)S(1)}, f32[3,4,128,128]{3,2,1,0:T(8,128)}, u32[]{:S(2)}) %copy-start) | copy-done | bytes 786456
  3.1 0.0 copy-start.1
  3.1 1.1 %copy-done.1 = f32[3,4,128,128]{3,2,1,0:T(8,128)S(1)} copy-done((f32[3,4,128,128]{3,2,1,0:T(8,128)S(1)}, f32[3,4,128,128]{3,2,1,0:T(8,128)}, u32[]{:S(2)}) %copy-start.1) | copy-done | bytes 786456
  4.2 0.0 copy-start.2
  4.2 0.9 %copy-done.2 = f32[4,128,128]{2,1,0:T(8,128)S(1)} copy-done((f32[4,128,128]{2,1,0:T(8,128)S(1)}, f32[4,128,128]{2,1,0:T(8,128)}, u32[]{:S(2)}) %copy-start.2) | copy-done | bytes 262168
  5.2 0.0 copy-start.3
  5.2 0.9 %copy-done.3 = f32[4,128,128]{2,1,0:T(8,128)S(1)} copy-done((f32[4,128,128]{2,1,0:T(8,128)S(1)}, f32[4,128,128]{2,1,0:T(8,128)}, u32[]{:S(2)}) %copy-start.3) | copy-done | bytes 262168
  6.1 0.0 copy-start.4
  6.1 0.9 %copy-done.4 = f32[4,128,128]{2,1,0:T(8,128)S(1)} copy-done((f32[4,128,128]{2,1,0:T(8,128)S(1)}, f32[4,128,128]{2,1,0:T(8,128)}, u32[]{:S(2)}) %copy-start.4) | copy-done | bytes 262168
  7.1 0.0 copy-start.5
  7.1 0.9 %copy-done.5 = f32[4,128,128]{2,1,0:T(8,128)S(1)} copy-done((f32[4,128,128]{2,1,0:T(8,128)S(1)}, f32[4,128,128]{2,1,0:T(8,128)}, u32[]{:S(2)}) %copy-start.5) | copy-done | bytes 262168
  8.0 0.0 copy-start.6
  8.0 0.9 %copy-done.6 = s32[4,128,128]{2,1,0:T(8,128)S(1)} copy-done((s32[4,128,128]{2,1,0:T(8,128)S(1)}, s32[4,128,128]{2,1,0:T(8,128)}, u32[]{:S(2)}) %copy-start.6) | copy-done | bytes 262168
  9.0 0.0 copy-start.8
  9.0 0.7 %copy-done.8 = s32[1,1,1,512]{3,2,1,0:T(1,128)S(1)} copy-done((s32[1,1,1,512]{3,2,1,0:T(1,128)S(1)}, s32[1,1,1,512]{3,2,1,0:T(1,128)}, u32[]{:S(2)}) %copy-start.8) | copy-done | bytes 2072
  9.7 0.0 copy-start.9
  9.7 0.7 %copy-done.9 = f32[1,1,1,512]{3,2,1,0:T(1,128)S(1)} copy-done((f32[1,1,1,512]{3,2,1,0:T(1,128)S(1)}, f32[1,1,1,512]{3,2,1,0:T(1,128)}, u32[]{:S(2)}) %copy-start.9) | copy-done | bytes 2072
  10.3 39.6 %shard_map.139 = (f32[4,128,128]{2,1,0:T(8,128)S(1)}, f32[3,4,128,128]{3,2,1,0:T(8,128)S(1)}, f32[8,64]{1,0:T(8,128)S(1)}) custom-call(f32[4,128,128]{2,1,0:T(8,128)S(1)} %copy-done.2, f32[3,4,128,128]{3,2,1,0:T(8,128)S(1)} %copy-done, f32[4,128,128]{2,1,0:T(8,128)S(1)} %copy-done.3, f32[4,128,128]{2,1,0:T(8,128)S(1)} %copy-done.4, ...), custom_call_target="tpu_custom_call" | custom-call | flops 1000000000 | bytes 4000000 | tf_op jit(solution)/shard_map/pallas_call | solution.py:339
  50.0 0.7 %copy.20 = f32[4,128,128]{2,1,0:T(8,128)} copy(f32[4,128,128]{2,1,0:T(8,128)S(1)} %get-tuple-element.6) | data formatting | bytes 524288
  50.7 0.9 %copy.21 = f32[3,4,128,128]{3,2,1,0:T(8,128)} copy(f32[3,4,128,128]{3,2,1,0:T(8,128)S(1)} %get-tuple-element.7) | data formatting | bytes 1572864
  51.5 0.6 %copy.22 = f32[8,64]{1,0:T(8,128)} copy(f32[8,64]{1,0:T(8,128)S(1)} %get-tuple-element.8) | data formatting | bytes 4096
Async XLA Ops:
  0.6 1.3 %copy-start.7 = (s32[1,1,1,512]{3,2,1,0:T(1,128)S(1)}, s32[1,1,1,512]{3,2,1,0:T(1,128)}, u32[]{:S(2)}) copy-start(s32[1,1,1,512]{3,2,1,0:T(1,128)} %cells_ref.1) | copy-start | bytes 6148
  2.0 1.1 %copy-start = (f32[3,4,128,128]{3,2,1,0:T(8,128)S(1)}, f32[3,4,128,128]{3,2,1,0:T(8,128)}, u32[]{:S(2)}) copy-start(f32[3,4,128,128]{3,2,1,0:T(8,128)} %v_in.1) | copy-start | bytes 2359300
  3.1 1.1 %copy-start.1 = (f32[3,4,128,128]{3,2,1,0:T(8,128)S(1)}, f32[3,4,128,128]{3,2,1,0:T(8,128)}, u32[]{:S(2)}) copy-start(f32[3,4,128,128]{3,2,1,0:T(8,128)} %av_in.1) | copy-start | bytes 2359300
  4.2 0.9 %copy-start.2 = (f32[4,128,128]{2,1,0:T(8,128)S(1)}, f32[4,128,128]{2,1,0:T(8,128)}, u32[]{:S(2)}) copy-start(f32[4,128,128]{2,1,0:T(8,128)} %p_in.1) | copy-start | bytes 786436
  5.2 0.9 %copy-start.3 = (f32[4,128,128]{2,1,0:T(8,128)S(1)}, f32[4,128,128]{2,1,0:T(8,128)}, u32[]{:S(2)}) copy-start(f32[4,128,128]{2,1,0:T(8,128)} %kap_in.1) | copy-start | bytes 786436
  6.1 0.9 %copy-start.4 = (f32[4,128,128]{2,1,0:T(8,128)S(1)}, f32[4,128,128]{2,1,0:T(8,128)}, u32[]{:S(2)}) copy-start(f32[4,128,128]{2,1,0:T(8,128)} %drv_in.1) | copy-start | bytes 786436
  7.1 0.9 %copy-start.5 = (f32[4,128,128]{2,1,0:T(8,128)S(1)}, f32[4,128,128]{2,1,0:T(8,128)}, u32[]{:S(2)}) copy-start(f32[4,128,128]{2,1,0:T(8,128)} %ap_in.1) | copy-start | bytes 786436
  8.0 0.9 %copy-start.6 = (s32[4,128,128]{2,1,0:T(8,128)S(1)}, s32[4,128,128]{2,1,0:T(8,128)}, u32[]{:S(2)}) copy-start(s32[4,128,128]{2,1,0:T(8,128)} %mask_in.1) | copy-start | bytes 786436
  9.0 0.7 %copy-start.8 = (s32[1,1,1,512]{3,2,1,0:T(1,128)S(1)}, s32[1,1,1,512]{3,2,1,0:T(1,128)}, u32[]{:S(2)}) copy-start(s32[1,1,1,512]{3,2,1,0:T(1,128)} %rows_ref.1) | copy-start | bytes 6148
  9.7 0.7 %copy-start.9 = (f32[1,1,1,512]{3,2,1,0:T(1,128)S(1)}, f32[1,1,1,512]{3,2,1,0:T(1,128)}, u32[]{:S(2)}) copy-start(f32[1,1,1,512]{3,2,1,0:T(1,128)} %angle_ref.1) | copy-start | bytes 6148

commit v2 on v1

v2 whole, which is shorter than its diff:
```python
import functools

import jax
import jax.numpy as jnp
from jax import lax
from jax.experimental import pallas as pl
from jax.experimental.pallas import tpu as pltpu
from jax.sharding import PartitionSpec as P

ANG = 64
CX = 4
CY = 128
CZ = 128
WALL = 512
OWN = 8
NXC = 4
NYC = 4
ZL = 4
ZH = 2
NA = NXC * NYC
NB = 2 * ZL * ZH
WIDTH = NB * OWN
MESH = pl.DeviceIdType.MESH
PLANE = sorted(
    ((dy, dx) for dy in range(NYC) for dx in range(NXC)),
    key=lambda d: (min(d[0], NYC - d[0]) + min(d[1], NXC - d[1]), d),
)
F32 = jnp.float32
BF16 = jnp.bfloat16


def pieces(value):
    high = value.astype(BF16)
    rest = value - high.astype(F32)
    mid = rest.astype(BF16)
    low = (rest - mid.astype(F32)).astype(BF16)
    return high, mid, low


def kernel(
    ns, nr, nc,
    p_in, v_in, kap_in, drv_in, ap_in, av_in, mask_in, cells_in, rows_in, angle_in, count_in, step_in,
    ap_out, av_out, grad_out,
    cells_ref, rows_ref, angle_ref, count_ref, step_ref,
    pp, qq, kap, drv, ap, vel, avel, mask,
    lam0, lam1, lam2, apo,
    zsend, zrecv, lsend, lrecv,
    slots, vals, hot, weight, where_hot, sens_t, dense, parts,
    small_sem, load_sem, store_sem, halo_send, halo_recv, lam_send, lam_recv,
    slot_send, slot_recv, val_send, val_recv, part_send, part_recv,
):
    s = lax.axis_index("slab")
    r = lax.axis_index("row")
    c = lax.axis_index("col")
    y, zl = lax.div(s, ZL), lax.rem(s, ZL)
    x_at, zh = lax.div(c, ZH), lax.rem(c, ZH)
    group = y * NXC + x_at
    b = (zl * 2 + r) * ZH + zh

    def plane_peer(k):
        dy, dx = PLANE[k]
        return (lax.rem(y + dy, NYC) * ZL + zl, r, lax.rem(x_at + dx, NXC) * ZH + zh)

    def line_peer(k):
        other_zl = lax.rem(zl + lax.div(k, 2 * ZH), ZL)
        other_r = lax.rem(r + lax.rem(lax.div(k, ZH), 2), 2)
        other_zh = lax.rem(zh + lax.rem(k, ZH), ZH)
        return (y * ZL + other_zl, other_r, x_at * ZH + other_zh)

    loads = [
        pltpu.make_async_copy(kap_in, kap, load_sem.at[0]),
        pltpu.make_async_copy(ap_in, ap, load_sem.at[1]),
        pltpu.make_async_copy(p_in, pp.at[pl.ds(1, CX), pl.ds(8, CY)], load_sem.at[2]),
        pltpu.make_async_copy(av_in, avel, load_sem.at[3]),
        pltpu.make_async_copy(mask_in, mask, load_sem.at[4]),
        pltpu.make_async_copy(v_in, vel, load_sem.at[5]),
        pltpu.make_async_copy(drv_in, drv, load_sem.at[6]),
    ]
    small = [
        pltpu.make_async_copy(rows_in, rows_ref, small_sem.at[0]),
        pltpu.make_async_copy(angle_in, angle_ref, small_sem.at[1]),
        pltpu.make_async_copy(count_in, count_ref, small_sem.at[2]),
        pltpu.make_async_copy(cells_in, cells_ref, small_sem.at[3]),
        pltpu.make_async_copy(step_in, step_ref, small_sem.at[4]),
    ]
    for copy in small + loads:
        copy.start()

    plane = jnp.zeros((CY, CZ), F32)
    for ref in (pp, qq):
        ref[0, pl.ds(8, CY)] = plane
        ref[CX + 1, pl.ds(8, CY)] = plane
        for x in range(CX):
            ref[x + 1, pl.ds(0, 8)] = jnp.zeros((8, CZ), F32)
            ref[x + 1, pl.ds(CY + 8, 8)] = jnp.zeros((8, CZ), F32)
    lam0[0] = plane
    lam0[CX + 1] = plane
    for x in range(CX):
        lam1[x, pl.ds(0, 8)] = jnp.zeros((8, CZ), F32)
        lam1[x, pl.ds(CY + 8, 8)] = jnp.zeros((8, CZ), F32)
    zrecv[...] = jnp.zeros_like(zrecv)
    lrecv[...] = jnp.zeros_like(lrecv)

    barrier = pltpu.get_barrier_semaphore()

    def greet(device):
        pl.semaphore_signal(barrier, inc=1, device_id=device, device_id_type=MESH)

    def greet_line(k, _):
        greet(line_peer(k))
        return 0

    s_up, s_down = jnp.minimum(s + 1, ns - 1), jnp.maximum(s - 1, 0)
    r_up, r_down = jnp.minimum(r + 1, nr - 1), jnp.maximum(r - 1, 0)
    c_up, c_down = jnp.minimum(c + 1, nc - 1), jnp.maximum(c - 1, 0)
    has = {
        "xu": s < ns - 1, "xd": s > 0, "yu": r < nr - 1, "yd": r > 0, "zu": c < nc - 1, "zd": c > 0,
    }
    beyond = (
        (jnp.logical_and(zh == ZH - 1, has["zu"]), (s, r, c_up)),
        (jnp.logical_and(zh == 0, has["zd"]), (s, r, c_down)),
        (jnp.logical_and(zl == ZL - 1, has["xu"]), (s_up, r, c)),
        (jnp.logical_and(zl == 0, has["xd"]), (s_down, r, c)),
    )
    partners = NA - 1 + NB - 1
    for here, device in beyond:
        pl.when(here)(functools.partial(greet, device))
        partners = partners + here.astype(jnp.int32)
    for k in range(1, NA):
        greet(plane_peer(k))
    lax.fori_loop(1, NB, greet_line, 0)

    lane = lax.broadcasted_iota(jnp.int32, (1, WALL), 1)
    for copy in small:
        copy.wait()
    own_rows = rows_ref[0, 0]
    live = lane < count_ref[0, 0, 0]
    bits = own_rows >> 3
    owner_group = ((bits >> 6) << 2) + ((bits >> 1) & 3)
    owner_line = (((bits >> 4) & 3) << 2) + (((bits >> 3) & 1) << 1) + (bits & 1)
    code = owner_group * WIDTH + owner_line * OWN + (own_rows & (OWN - 1))
    slots[0, 0:1] = jnp.where(live, code.astype(F32), -1.0)
    slots[0, 1:2] = angle_ref[0, 0]
    row_at = (lax.broadcasted_iota(jnp.int32, (WIDTH, WALL), 0) + group * WIDTH).astype(F32)
    knots = lax.broadcasted_iota(jnp.int32, (ANG, WALL), 0).astype(F32)

    def prepare(k):
        hot[k] = jnp.where(slots[k, 0:1] == row_at, 1.0, 0.0).astype(BF16)
        dist = jnp.abs(slots[k, 1:2] - knots)
        dist = jnp.minimum(dist, ANG - dist)
        outer = jnp.maximum(2.0 - dist, 0.0)
        near = jnp.maximum(1.0 - dist, 0.0)
        weight[k] = (outer * outer * outer - 4.0 * near * near * near) * (1.0 / 6.0)

    prepare(0)

    own_cells = cells_ref[0, 0]
    own_xy = own_cells >> 7
    own_z = own_cells & (CZ - 1)
    xy = lax.broadcasted_iota(jnp.int32, (CY, WALL), 0)
    for x in range(CX):
        where_hot[x * CY:(x + 1) * CY] = jnp.where(xy + x * CY == own_xy, 1.0, 0.0).astype(BF16)

    loads[0].wait()
    loads[1].wait()
    rows_of = pl.ds(8, CY)
    for x in range(CX):
        qq[x + 1, rows_of] = kap[x] * ap[x]
    loads[2].wait()
    for ref, at in ((pp, 0), (qq, CX)):
        for x in range(CX):
            turned = ref[x + 1, rows_of].T
            zsend[at + x:at + x + 1] = turned[0:1]
            zsend[8 + at + x:8 + at + x + 1] = turned[CZ - 1:CZ]

    pl.semaphore_wait(barrier, partners)

    def slot_copy(k):
        return pltpu.make_async_remote_copy(
            src_ref=slots.at[0], dst_ref=slots.at[k],
            send_sem=slot_send, recv_sem=slot_recv.at[k],
            device_id=plane_peer(k), device_id_type=MESH,
        )

    def halo(src, dst, sem_at, send_sem, recv_sem, device):
        return pltpu.make_async_remote_copy(
            src_ref=src, dst_ref=dst, send_sem=send_sem.at[sem_at], recv_sem=recv_sem.at[sem_at],
            device_id=device, device_id_type=MESH,
        )


    def field_x(ref, base):
        return {
            "xu": halo(ref.at[CX, rows_of], ref.at[0, rows_of], base, halo_send, halo_recv, (s_up, r, c)),
            "xd": halo(ref.at[1, rows_of], ref.at[CX + 1, rows_of], base + 1, halo_send, halo_recv, (s_down, r, c)),
        }

    def field_y(ref, base):
        inner = pl.ds(1, CX)
        return {
            "yu": halo(ref.at[inner, pl.ds(CY, 8)], ref.at[inner, pl.ds(0, 8)], base, halo_send, halo_recv, (s, r_up, c)),
            "yd": halo(ref.at[inner, pl.ds(8, 8)], ref.at[inner, pl.ds(CY + 8, 8)], base + 1, halo_send, halo_recv, (s, r_down, c)),
        }

    q_x = field_x(qq, 0)
    p_x = field_x(pp, 2)
    q_y = field_y(qq, 4)
    p_y = field_y(pp, 6)
    pq_z = {
        "zu": halo(zsend.at[pl.ds(8, 8)], zrecv.at[pl.ds(0, 8)], 8, halo_send, halo_recv, (s, r, c_up)),
        "zd": halo(zsend.at[pl.ds(0, 8)], zrecv.at[pl.ds(8, 8)], 9, halo_send, halo_recv, (s, r, c_down)),
    }
    inner = pl.ds(0, CX)
    lam_x = {
        "xu": halo(lam0.at[CX], lam0.at[0], 0, lam_send, lam_recv, (s_up, r, c)),
        "xd": halo(lam0.at[1], lam0.at[CX + 1], 1, lam_send, lam_recv, (s_down, r, c)),
    }
    lam_y = {
        "yu": halo(lam1.at[inner, pl.ds(CY, 8)], lam1.at[inner, pl.ds(0, 8)], 2, lam_send, lam_recv, (s, r_up, c)),
        "yd": halo(lam1.at[inner, pl.ds(8, 8)], lam1.at[inner, pl.ds(CY + 8, 8)], 3, lam_send, lam_recv, (s, r_down, c)),
    }
    lam_z = {
        "zu": halo(lsend.at[pl.ds(8, 8)], lrecv.at[pl.ds(0, 8)], 4, lam_send, lam_recv, (s, r, c_up)),
        "zd": halo(lsend.at[pl.ds(0, 8)], lrecv.at[pl.ds(8, 8)], 5, lam_send, lam_recv, (s, r, c_down)),
    }

    def start(faces):
        for side, copy in faces.items():
            pl.when(has[side])(copy.start)

    opposite = {"xu": "xd", "xd": "xu", "yu": "yd", "yd": "yu", "zu": "zd", "zd": "zu"}

    def arrive(faces):
        for side, copy in faces.items():
            pl.when(has[opposite[side]])(copy.wait_recv)

    def sent(faces):
        for side, copy in faces.items():
            pl.when(has[side])(copy.wait_send)

    start(pq_z)
    for k in range(NA - 1, 0, -1):
        slot_copy(k).start()
    start(q_x)
    start(p_x)
    start(q_y)
    start(p_y)
    halos = [q_x, q_y, p_x, p_y, pq_z]

    def slots_of(k, _):
        pltpu.make_async_copy(slots.at[k], slots.at[k], slot_recv.at[k]).wait()
        prepare(k)
        return 0

    lax.fori_loop(1, NA, slots_of, 0)
    rest = slots.at[pl.ds(1, NA - 1)]

    phase = jnp.cos(0.5 * jnp.full((1, CZ), lax.rem(step_ref[0], 97).astype(F32), F32))
    for copy in loads[3:]:
        copy.wait()
    for faces in (q_x, q_y, p_x, p_y, pq_z):
        arrive(faces)
    edge_t = jnp.concatenate([zrecv[...], jnp.zeros((CZ - 16, CZ), F32)], axis=0).T
    at_z = lax.broadcasted_iota(jnp.int32, (CY, CZ), 1)

    def along_z(field, low, high):
        upper = jnp.where(at_z == CZ - 1, high, pltpu.roll(field, CZ - 1, 1))
        lower = jnp.where(at_z == 0, low, pltpu.roll(field, 1, 1))
        return (upper - lower) * 0.5

    def slopes(ref, x, at):
        mid = ref[x + 1, rows_of]
        return (
            (ref[x + 2, rows_of] - ref[x, rows_of]) * 0.5,
            (ref[x + 1, pl.ds(9, CY)] - ref[x + 1, pl.ds(7, CY)]) * 0.5,
            along_z(mid, edge_t[:, at + x:at + x + 1], edge_t[:, 8 + at + x:8 + at + x + 1]),
        )

    for x in range(CX):
        dp = slopes(pp, x, 0)
        dq = slopes(qq, x, CX)
        free = 1.0 - mask[x].astype(F32)
        total = [avel[k, x] + dq[k] for k in range(3)]
        lam0[x + 1] = free * total[0]
        lam1[x, rows_of] = free * total[1]
        lam2[x] = free * total[2]
        sens = -(
            total[0] * (vel[0, x] - 0.3 * dp[0] + drv[x] * phase)
            + total[1] * (vel[1, x] - 0.3 * dp[1])
            + total[2] * (vel[2, x] - 0.3 * dp[2])
        )
        for i, piece in enumerate(pieces(sens.T)):
            sens_t[i * CZ:(i + 1) * CZ, x * CY:(x + 1) * CY] = piece

    picked = jnp.dot(sens_t[...], where_hot[...], preferred_element_type=F32)
    picked = picked[0:CZ] + picked[CZ:2 * CZ] + picked[2 * CZ:3 * CZ]
    z_at = lax.broadcasted_iota(jnp.int32, (CZ, WALL), 0)
    vals[0] = jnp.sum(jnp.where(z_at == own_z, picked, 0.0), axis=0, keepdims=True)

    for k in range(NA - 1, 0, -1):
        pltpu.make_async_remote_copy(
            src_ref=vals.at[0], dst_ref=vals.at[k], send_sem=val_send, recv_sem=val_recv.at[k],
            device_id=plane_peer(k), device_id_type=MESH,
        ).start()

    start(lam_x)
    start(lam_y)
    for x in range(CX):
        turned = lam2[x].T
        lsend[x:x + 1] = turned[0:1]
        lsend[8 + x:9 + x] = turned[CZ - 1:CZ]
    start(lam_z)
    stores = [
        pltpu.make_async_copy(lam0.at[pl.ds(1, CX)], av_out.at[0], store_sem.at[0]),
        pltpu.make_async_copy(lam1.at[pl.ds(0, CX), rows_of], av_out.at[1], store_sem.at[1]),
        pltpu.make_async_copy(lam2, av_out.at[2], store_sem.at[2]),
    ]
    for copy in stores:
        copy.start()

    def product(k):
        scaled = jnp.concatenate(pieces(weight[k] * vals[k]), axis=0)
        return lax.dot_general(hot[k], scaled, (((1,), (1,)), ((), ())), preferred_element_type=F32)

    def add_up(k, total):
        pltpu.make_async_copy(vals.at[k], vals.at[k], val_recv.at[k]).wait()
        return total + product(k)

    rest_vals = vals.at[pl.ds(1, NA - 1)]
    summed = lax.fori_loop(1, NA, add_up, product(0))
    summed = summed[:, 0:ANG] + summed[:, ANG:2 * ANG] + summed[:, 2 * ANG:3 * ANG]
    dense[...] = jnp.concatenate([summed, jnp.zeros_like(summed)], axis=1).reshape(NB, OWN, 2 * ANG)

    def send_part(k, _):
        peer = line_peer(k)
        other = (lax.rem(peer[0], ZL) * 2 + peer[1]) * ZH + lax.rem(peer[2], ZH)
        pltpu.make_async_remote_copy(
            src_ref=dense.at[other], dst_ref=parts.at[k - 1], send_sem=part_send, recv_sem=part_recv,
            device_id=peer, device_id_type=MESH,
        ).start()
        return 0

    lax.fori_loop(1, NB, send_part, 0)

    for faces in (lam_x, lam_y, lam_z):
        arrive(faces)
    edge_l = jnp.concatenate([lrecv[...], jnp.zeros((CZ - 16, CZ), F32)], axis=0).T
    for x in range(CX):
        div = (
            (lam0[x + 2] - lam0[x]) * 0.5
            + (lam1[x, pl.ds(9, CY)] - lam1[x, pl.ds(7, CY)]) * 0.5
            + along_z(lam2[x], edge_l[:, x:x + 1], edge_l[:, 8 + x:9 + x])
        )
        apo[x] = ap[x] + 0.3 * div
    last = pltpu.make_async_copy(apo, ap_out, store_sem.at[3])
    last.start()

    pltpu.make_async_copy(parts, parts, part_recv).wait()
    grad_out[...] = (dense[b] + jnp.sum(parts[...], axis=0))[:, 0:ANG]

    for faces in (q_x, q_y, p_x, p_y, pq_z, lam_x, lam_y, lam_z):
        sent(faces)
    pltpu.make_async_copy(rest, rest, slot_send).wait()
    pltpu.make_async_copy(rest_vals, rest_vals, val_send).wait()
    pltpu.make_async_copy(parts, parts, part_send).wait()
    for copy in stores + [last]:
        copy.wait()


def local(ns, nr, nc, *args):
    hbm = pl.BlockSpec(memory_space=pltpu.HBM)
    vmem = pl.BlockSpec(memory_space=pltpu.VMEM)
    block = (CX, CY, CZ)
    dma = pltpu.SemaphoreType.DMA
    return pl.pallas_call(
        functools.partial(kernel, ns, nr, nc),
        out_shape=(
            jax.ShapeDtypeStruct(block, F32),
            jax.ShapeDtypeStruct((3,) + block, F32),
            jax.ShapeDtypeStruct((OWN, ANG), F32),
        ),
        in_specs=[hbm] * 12,
        out_specs=(pl.BlockSpec(memory_space=pl.ANY), pl.BlockSpec(memory_space=pl.ANY), vmem),
        scratch_shapes=[
            pltpu.VMEM((1, 1, 1, WALL), jnp.int32),
            pltpu.VMEM((1, 1, 1, WALL), jnp.int32),
            pltpu.VMEM((1, 1, 1, WALL), F32),
            pltpu.SMEM((1, 1, 1), jnp.int32),
            pltpu.SMEM((1,), jnp.int32),
            pltpu.VMEM((CX + 2, CY + 16, CZ), F32),
            pltpu.VMEM((CX + 2, CY + 16, CZ), F32),
            pltpu.VMEM(block, F32),
            pltpu.VMEM(block, F32),
            pltpu.VMEM(block, F32),
            pltpu.VMEM((3,) + block, F32),
            pltpu.VMEM((3,) + block, F32),
            pltpu.VMEM(block, jnp.int32),
            pltpu.VMEM((CX + 2, CY, CZ), F32),
            pltpu.VMEM((CX, CY + 16, CZ), F32),
            pltpu.VMEM(block, F32),
            pltpu.VMEM(block, F32),
            pltpu.VMEM((16, CY), F32),
            pltpu.VMEM((16, CY), F32),
            pltpu.VMEM((16, CY), F32),
            pltpu.VMEM((16, CY), F32),
            pltpu.VMEM((NA, 2, WALL), F32),
            pltpu.VMEM((NA, 1, WALL), F32),
            pltpu.VMEM((NA, WIDTH, WALL), BF16),
            pltpu.VMEM((NA, ANG, WALL), F32),
            pltpu.VMEM((CX * CY, WALL), BF16),
            pltpu.VMEM((3 * CZ, CX * CY), BF16),
            pltpu.VMEM((NB, OWN, 2 * ANG), F32),
            pltpu.VMEM((NB - 1, OWN, 2 * ANG), F32),
            dma((5,)), dma((7,)), dma((4,)), dma((10,)), dma((10,)), dma((6,)), dma((6,)),
            dma, dma((NA,)), dma, dma((NA,)), dma, dma,
        ],
        compiler_params=pltpu.CompilerParams(
            collective_id=0, has_side_effects=True, vmem_limit_bytes=60 * 1024 * 1024
        ),
        cost_estimate=pl.CostEstimate(flops=10**9, bytes_accessed=4 * 10**6, transcendentals=0),
    )(*args)


def solution(mesh):
    names = ("slab", "row", "col")
    sizes = tuple(mesh.shape[name] for name in names)
    cells = P(*names)
    vector = P(None, *names)
    slot = P(*names, None)
    in_specs = (cells, vector, cells, cells, cells, vector, cells, slot, slot, slot, cells, P())
    out_specs = (cells, vector, P(names, None))
    return jax.shard_map(
        functools.partial(local, *sizes), mesh=mesh, in_specs=in_specs, out_specs=out_specs, check_vma=False
    )
```

time: 52.5 us -> 39 us (0.74)
  Pallas kernels: 39.6 us -> 32.5 us
  local copies, waits for them, and re-layouts: 10.5 us -> 4.33 us
    pallas_call x1, Pallas kernels: 39.6 us -> 32.5 us  [local(): pl.pallas_call(functools.partial(kernel, ns, nr, nc), out_shape=(jax.Shap...]
    unnamed x23 -> x5, local copies, waits for them, and re-layouts: 10.5 us -> 4.33 us
where the time goes in v2:
time: 39 us; the launch traced here: 38.8 us
  Pallas kernels  32.5 us (83%)
  local copies, waits for them, and re-layouts  4.33 us (11%)
  between operations  1.94 us (5%)
    pallas_call x1, Pallas kernels, local(): pl.pallas_call(functools.partial(kernel, ns, nr, nc), out_shape=(jax.Shap...  32.5 us
    unnamed x5, local copies, waits for them, and re-layouts  4.33 us

profile of v2, /device:TPU:1, one launch (start us, length us, event | category | flops | bytes accessed | tf_op | source)
XLA Modules:
  0.0 38.8 jit_solution(14875365475005746223)
XLA Ops:
  1.9 32.5 %shard_map.139 = (f32[4,128,128]{2,1,0:T(8,128)}, f32[3,4,128,128]{3,2,1,0:T(8,128)}, f32[8,64]{1,0:T(8,128)}) custom-call(f32[4,128,128]{2,1,0:T(8,128)} %p_in.1, f32[3,4,128,128]{3,2,1,0:T(8,128)} %v_in.1, f32[4,128,128]{2,1,0:T(8,128)} %kap_in.1, f32[4,128,128]{2,1,0:T(8,128)} %drv_in.1, f32[4,128,128]{2,1,0:T(8,128)} %ap_in.1, f32[3,4,128,128]{3,2,1,0:T(8,128)} %av_in.1, ...), custom_call_target="tpu_custom_call" | custom-call | flops 1000000000 | bytes 4000000 | tf_op jit(solution)/shard_map/pallas_call | solution.py:375
  34.5 1.7 %copy.20 = f32[4,128,128]{2,1,0:T(8,128)} copy(f32[4,128,128]{2,1,0:T(8,128)} %get-tuple-element.6) | data formatting | bytes 524288
  36.1 0.0 copy-start
  36.1 2.1 %copy.21 = f32[3,4,128,128]{3,2,1,0:T(8,128)} copy(f32[3,4,128,128]{3,2,1,0:T(8,128)} %get-tuple-element.7) | data formatting | bytes 1572864
  38.2 0.0 copy-done
  38.2 0.6 %copy.22 = f32[8,64]{1,0:T(8,128)} copy(f32[8,64]{1,0:T(8,128)S(1)} %copy-done) | data formatting | bytes 4096
Async XLA Ops:
  36.1 2.1 %copy-start = (f32[8,64]{1,0:T(8,128)S(1)}, f32[8,64]{1,0:T(8,128)}, u32[]{:S(2)}) copy-start(f32[8,64]{1,0:T(8,128)} %get-tuple-element.8) | copy-start | bytes 6148

commit v3 on v2

--- a/solution.py
+++ b/solution.py
@@ -367,17 +367,37 @@
         copy.wait()
 
 
+def written(outs):
+    anyspace = pl.BlockSpec(memory_space=pl.ANY)
+    return pl.pallas_call(
+        hand3,
+        out_shape=tuple(jax.ShapeDtypeStruct(o.shape, o.dtype) for o in outs),
+        in_specs=[anyspace] * 3,
+        out_specs=(anyspace,) * 3,
+        scratch_shapes=[pltpu.SemaphoreType.DMA((3,))],
+        compiler_params=pltpu.CompilerParams(vmem_limit_bytes=1024 * 1024),
+    )(*outs)
+
+
+def hand3(a, b, c, d, e, f, sem):
+    copies = [pltpu.make_async_copy(x, y, sem.at[i]) for i, (x, y) in enumerate(((a, d), (b, e), (c, f)))]
+    for copy in copies:
+        copy.start()
+    for copy in copies:
+        copy.wait()
+
+
 def local(ns, nr, nc, *args):
     hbm = pl.BlockSpec(memory_space=pltpu.HBM)
     vmem = pl.BlockSpec(memory_space=pltpu.VMEM)
     block = (CX, CY, CZ)
     dma = pltpu.SemaphoreType.DMA
-    return pl.pallas_call(
+    return written(pl.pallas_call(
         functools.partial(kernel, ns, nr, nc),
         out_shape=(
-            jax.ShapeDtypeStruct(block, F32),
-            jax.ShapeDtypeStruct((3,) + block, F32),
-            jax.ShapeDtypeStruct((OWN, ANG), F32),
+            pltpu.VMEM(block, F32),
+            pltpu.VMEM((3,) + block, F32),
+            pltpu.VMEM((OWN, ANG), F32),
         ),
         in_specs=[hbm] * 12,
         out_specs=(pl.BlockSpec(memory_space=pl.ANY), pl.BlockSpec(memory_space=pl.ANY), vmem),
@@ -415,10 +435,10 @@
             dma, dma((NA,)), dma, dma((NA,)), dma, dma,
         ],
         compiler_params=pltpu.CompilerParams(
-            collective_id=0, has_side_effects=True, vmem_limit_bytes=60 * 1024 * 1024
+            collective_id=0, has_side_effects=True, vmem_limit_bytes=62 * 1024 * 1024 + 512 * 1024
         ),
         cost_estimate=pl.CostEstimate(flops=10**9, bytes_accessed=4 * 10**6, transcendentals=0),
-    )(*args)
+    )(*args))
 
 
 def solution(mesh):

time: 39 us -> 35 us (0.90)
  local copies, waits for them, and re-layouts: 4.33 us -> 0 us
  Pallas kernels: 32.5 us -> 32.9 us
    unnamed x5 -> x0, local copies, waits for them, and re-layouts: 4.33 us -> none
    pallas_call x1 -> x2, Pallas kernels: 32.5 us -> 32.9 us  [the longest x1 31.9 us: local(): pl.pallas_call(functools.partial(kernel, ns, nr, nc), out_shape=(pltpu.VM...]
where the time goes in v3:
time: 35 us; the launch traced here: 34.9 us
  Pallas kernels  32.9 us (94%)
  between operations  1.93 us (6%)
    pallas_call x1, Pallas kernels, local(): pl.pallas_call(functools.partial(kernel, ns, nr, nc), out_shape=(pltpu.VM...  31.9 us
    pallas_call x1, Pallas kernels, written(): pl.pallas_call(hand3, out_shape=tuple((jax.ShapeDtypeStruct(o.shape, o.dt...  1 us

profile of v3, /device:TPU:1, one launch (start us, length us, event | category | flops | bytes accessed | tf_op | source)
XLA Modules:
  0.0 34.9 jit_solution(455315981784074005)
XLA Ops:
  1.9 31.9 %shard_map.139 = (f32[4,128,128]{2,1,0:T(8,128)S(1)}, f32[3,4,128,128]{3,2,1,0:T(8,128)S(1)}, f32[8,64]{1,0:T(8,128)S(1)}) custom-call(f32[4,128,128]{2,1,0:T(8,128)} %p_in.1, f32[3,4,128,128]{3,2,1,0:T(8,128)} %v_in.1, f32[4,128,128]{2,1,0:T(8,128)} %kap_in.1, f32[4,128,128]{2,1,0:T(8,128)} %drv_in.1, f32[4,128,128]{2,1,0:T(8,128)} %ap_in.1, ...), custom_call_target="tpu_custom_call" | custom-call | flops 1000000000 | bytes 4000000 | tf_op jit(solution)/shard_map/pallas_call | solution.py:395
  33.9 1.0 %shard_map.140 = (f32[4,128,128]{2,1,0:T(8,128)}, f32[3,4,128,128]{3,2,1,0:T(8,128)}, f32[8,64]{1,0:T(8,128)}) custom-call(f32[4,128,128]{2,1,0:T(8,128)S(1)} %get-tuple-element.6.a, f32[3,4,128,128]{3,2,1,0:T(8,128)S(1)} %get-tuple-element.7.b, f32[8,64]{1,0:T(8,128)S(1)} %get-tuple-element.8.c), custom_call_target="tpu_custom_call" | custom-call | tf_op jit(solution)/shard_map/pallas_call | solution.py:372

commit v4 on v3

--- a/solution.py
+++ b/solution.py
@@ -20,6 +20,7 @@
 NA = NXC * NYC
 NB = 2 * ZL * ZH
 WIDTH = NB * OWN
+BATCHES = (0, 5, 11, 16)
 MESH = pl.DeviceIdType.MESH
 PLANE = sorted(
     ((dy, dx) for dy in range(NYC) for dx in range(NXC)),
@@ -42,11 +43,14 @@
     p_in, v_in, kap_in, drv_in, ap_in, av_in, mask_in, cells_in, rows_in, angle_in, count_in, step_in,
     ap_out, av_out, grad_out,
     cells_ref, rows_ref, angle_ref, count_ref, step_ref,
-    pp, qq, kap, drv, ap, vel, avel, mask,
-    lam0, lam1, lam2, apo,
+    pp, qq, kap, drv, ap, vel, total, mask,
+    lam0, lam1, lam2, apo, sums, q_near,
     zsend, zrecv, lsend, lrecv,
+    turned_face, turned_wrap, face_parts, wrap_parts, slot_parts,
+    cells_buf, answer, answered,
     slots, vals, hot, weight, where_hot, sens_t, dense, parts,
     small_sem, load_sem, store_sem, halo_send, halo_recv, lam_send, lam_recv,
+    wrap_send, wrap_recv, cell_send, cell_recv, answer_send, answer_recv,
     slot_send, slot_recv, val_send, val_recv, part_send, part_recv,
 ):
     s = lax.axis_index("slab")
@@ -70,8 +74,8 @@
     loads = [
         pltpu.make_async_copy(kap_in, kap, load_sem.at[0]),
         pltpu.make_async_copy(ap_in, ap, load_sem.at[1]),
-        pltpu.make_async_copy(p_in, pp.at[pl.ds(1, CX), pl.ds(8, CY)], load_sem.at[2]),
-        pltpu.make_async_copy(av_in, avel, load_sem.at[3]),
+        pltpu.make_async_copy(p_in, pp.at[pl.ds(0, CX), pl.ds(8, CY)], load_sem.at[2]),
+        pltpu.make_async_copy(av_in, total, load_sem.at[3]),
         pltpu.make_async_copy(mask_in, mask, load_sem.at[4]),
         pltpu.make_async_copy(v_in, vel, load_sem.at[5]),
         pltpu.make_async_copy(drv_in, drv, load_sem.at[6]),
@@ -87,19 +91,19 @@
         copy.start()
 
     plane = jnp.zeros((CY, CZ), F32)
-    for ref in (pp, qq):
-        ref[0, pl.ds(8, CY)] = plane
-        ref[CX + 1, pl.ds(8, CY)] = plane
+    strip = jnp.zeros((8, CZ), F32)
+    for ref in (pp, qq, lam1):
         for x in range(CX):
-            ref[x + 1, pl.ds(0, 8)] = jnp.zeros((8, CZ), F32)
-            ref[x + 1, pl.ds(CY + 8, 8)] = jnp.zeros((8, CZ), F32)
+            ref[x, pl.ds(0, 8)] = strip
+            ref[x, pl.ds(CY + 8, 8)] = strip
+    for ref in (q_near, ):
+        ref[0] = plane
+        ref[1] = plane
     lam0[0] = plane
     lam0[CX + 1] = plane
-    for x in range(CX):
-        lam1[x, pl.ds(0, 8)] = jnp.zeros((8, CZ), F32)
-        lam1[x, pl.ds(CY + 8, 8)] = jnp.zeros((8, CZ), F32)
     zrecv[...] = jnp.zeros_like(zrecv)
     lrecv[...] = jnp.zeros_like(lrecv)
+    answered[...] = jnp.zeros_like(answered)
 
     barrier = pltpu.get_barrier_semaphore()
 
@@ -116,11 +120,15 @@
     has = {
         "xu": s < ns - 1, "xd": s > 0, "yu": r < nr - 1, "yd": r > 0, "zu": c < nc - 1, "zd": c > 0,
     }
+    wrap_up = jnp.logical_and(zl == ZL - 1, has["xu"])
+    wrap_down = jnp.logical_and(zl == 0, has["xd"])
+    near_up = zl < ZL - 1
+    near_down = zl > 0
     beyond = (
         (jnp.logical_and(zh == ZH - 1, has["zu"]), (s, r, c_up)),
         (jnp.logical_and(zh == 0, has["zd"]), (s, r, c_down)),
-        (jnp.logical_and(zl == ZL - 1, has["xu"]), (s_up, r, c)),
-        (jnp.logical_and(zl == 0, has["xd"]), (s_down, r, c)),
+        (wrap_up, (s_up, r, c)),
+        (wrap_down, (s_down, r, c)),
     )
     partners = NA - 1 + NB - 1
     for here, device in beyond:
@@ -144,8 +152,11 @@
     row_at = (lax.broadcasted_iota(jnp.int32, (WIDTH, WALL), 0) + group * WIDTH).astype(F32)
     knots = lax.broadcasted_iota(jnp.int32, (ANG, WALL), 0).astype(F32)
 
+    def at_slots(k):
+        return pl.ds(pl.multiple_of(k * WALL, WALL), WALL)
+
     def prepare(k):
-        hot[k] = jnp.where(slots[k, 0:1] == row_at, 1.0, 0.0).astype(BF16)
+        hot[:, at_slots(k)] = jnp.where(slots[k, 0:1] == row_at, 1.0, 0.0).astype(BF16)
         dist = jnp.abs(slots[k, 1:2] - knots)
         dist = jnp.minimum(dist, ANG - dist)
         outer = jnp.maximum(2.0 - dist, 0.0)
@@ -155,23 +166,47 @@
     prepare(0)
 
     own_cells = cells_ref[0, 0]
+    cells_buf[0] = own_cells
     own_xy = own_cells >> 7
+    own_x = own_cells >> 14
     own_z = own_cells & (CZ - 1)
-    xy = lax.broadcasted_iota(jnp.int32, (CY, WALL), 0)
+    y_at = lax.broadcasted_iota(jnp.int32, (CY, WALL), 0)
     for x in range(CX):
-        where_hot[x * CY:(x + 1) * CY] = jnp.where(xy + x * CY == own_xy, 1.0, 0.0).astype(BF16)
+        where_hot[x * CY:(x + 1) * CY] = jnp.where(y_at + x * CY == own_xy, 1.0, 0.0).astype(BF16)
 
     loads[0].wait()
     loads[1].wait()
     rows_of = pl.ds(8, CY)
     for x in range(CX):
-        qq[x + 1, rows_of] = kap[x] * ap[x]
+        qq[x, rows_of] = kap[x] * ap[x]
     loads[2].wait()
-    for ref, at in ((pp, 0), (qq, CX)):
+    for i, (ref, at) in enumerate(((pp, 0), (qq, CX))):
         for x in range(CX):
-            turned = ref[x + 1, rows_of].T
+            turned = ref[x, rows_of].T
             zsend[at + x:at + x + 1] = turned[0:1]
             zsend[8 + at + x:8 + at + x + 1] = turned[CZ - 1:CZ]
+            if x in (0, CX - 1):
+                turned_face[x // (CX - 1), i] = turned
+
+    def split_into(ref, first, second):
+        for i, field in enumerate((first, second)):
+            for j, piece in enumerate(pieces(field)):
+                ref[(3 * i + j) * CZ:(3 * i + j + 1) * CZ] = piece
+
+    for side in range(2):
+        split_into(face_parts.at[side], turned_face[side, 0], turned_face[side, 1])
+
+    def pick(ref, hot_y, at_z):
+        got = jnp.dot(ref[...], hot_y, preferred_element_type=F32)
+        out = []
+        for i in range(2):
+            field = got[3 * i * CZ:(3 * i + 1) * CZ]
+            field = field + got[(3 * i + 1) * CZ:(3 * i + 2) * CZ] + got[(3 * i + 2) * CZ:(3 * i + 3) * CZ]
+            out.append(jnp.sum(jnp.where(y_at == at_z, field, 0.0), axis=0, keepdims=True))
+        return out
+
+    def hot_y_of(cells):
+        return jnp.where(y_at == ((cells >> 7) & (CY - 1)), 1.0, 0.0).astype(BF16)
 
     pl.semaphore_wait(barrier, partners)
 
@@ -189,28 +224,36 @@
         )
 
 
-    def field_x(ref, base):
-        return {
-            "xu": halo(ref.at[CX, rows_of], ref.at[0, rows_of], base, halo_send, halo_recv, (s_up, r, c)),
-            "xd": halo(ref.at[1, rows_of], ref.at[CX + 1, rows_of], base + 1, halo_send, halo_recv, (s_down, r, c)),
-        }
+    inner = pl.ds(0, CX)
+    q_x = {
+        "xu": halo(qq.at[CX - 1, rows_of], q_near.at[0], 0, halo_send, halo_recv, (s_up, r, c)),
+        "xd": halo(qq.at[0, rows_of], q_near.at[1], 1, halo_send, halo_recv, (s_down, r, c)),
+    }
 
     def field_y(ref, base):
-        inner = pl.ds(1, CX)
         return {
             "yu": halo(ref.at[inner, pl.ds(CY, 8)], ref.at[inner, pl.ds(0, 8)], base, halo_send, halo_recv, (s, r_up, c)),
             "yd": halo(ref.at[inner, pl.ds(8, 8)], ref.at[inner, pl.ds(CY + 8, 8)], base + 1, halo_send, halo_recv, (s, r_down, c)),
         }
 
-    q_x = field_x(qq, 0)
-    p_x = field_x(pp, 2)
     q_y = field_y(qq, 4)
     p_y = field_y(pp, 6)
+    wrap = {
+        "xu": halo(turned_face.at[1], turned_wrap, 0, wrap_send, wrap_recv, (s_up, r, c)),
+        "xd": halo(turned_face.at[0], turned_wrap, 1, wrap_send, wrap_recv, (s_down, r, c)),
+    }
+    ask = {
+        "xu": halo(cells_buf.at[0], cells_buf.at[1], 0, cell_send, cell_recv, (s_up, r, c)),
+        "xd": halo(cells_buf.at[0], cells_buf.at[2], 1, cell_send, cell_recv, (s_down, r, c)),
+    }
+    reply = {
+        "xu": halo(answer.at[1], answered.at[0], 0, answer_send, answer_recv, (s_up, r, c)),
+        "xd": halo(answer.at[0], answered.at[1], 1, answer_send, answer_recv, (s_down, r, c)),
+    }
     pq_z = {
         "zu": halo(zsend.at[pl.ds(8, 8)], zrecv.at[pl.ds(0, 8)], 8, halo_send, halo_recv, (s, r, c_up)),
         "zd": halo(zsend.at[pl.ds(0, 8)], zrecv.at[pl.ds(8, 8)], 9, halo_send, halo_recv, (s, r, c_down)),
     }
-    inner = pl.ds(0, CX)
     lam_x = {
         "xu": halo(lam0.at[CX], lam0.at[0], 0, lam_send, lam_recv, (s_up, r, c)),
         "xd": halo(lam0.at[1], lam0.at[CX + 1], 1, lam_send, lam_recv, (s_down, r, c)),
@@ -238,28 +281,77 @@
         for side, copy in faces.items():
             pl.when(has[side])(copy.wait_send)
 
+    pl.when(wrap_up)(wrap["xu"].start)
+    pl.when(wrap_down)(wrap["xd"].start)
     start(pq_z)
+    pl.when(near_up)(ask["xu"].start)
+    pl.when(near_down)(ask["xd"].start)
+    start(q_y)
+    start(p_y)
     for k in range(NA - 1, 0, -1):
         slot_copy(k).start()
-    start(q_x)
-    start(p_x)
-    start(q_y)
-    start(p_y)
-    halos = [q_x, q_y, p_x, p_y, pq_z]
+
+    phase = jnp.cos(0.5 * jnp.full((1, CZ), lax.rem(step_ref[0], 97).astype(F32), F32))
+    for copy in loads[3:]:
+        copy.wait()
+    arrive(q_y)
+    arrive(p_y)
+
+    def along_x(ref, x):
+        if x == 0:
+            return ref[1, rows_of] * 0.5
+        if x == CX - 1:
+            return ref[CX - 2, rows_of] * -0.5
+        return (ref[x + 1, rows_of] - ref[x - 1, rows_of]) * 0.5
+
+    def along_y(ref, x):
+        return (ref[x, pl.ds(9, CY)] - ref[x, pl.ds(7, CY)]) * 0.5
+
+    for x in range(CX):
+        total_0 = total[0, x] + along_x(qq, x)
+        total_1 = total[1, x] + along_y(qq, x)
+        total[0, x] = total_0
+        total[1, x] = total_1
+        moved_0 = vel[0, x] - 0.3 * along_x(pp, x) + drv[x] * phase
+        sums[x] = total_0 * moved_0 + total_1 * (vel[1, x] - 0.3 * along_y(pp, x))
+        if x in (0, CX - 1):
+            split_into(slot_parts.at[x // (CX - 1)], total_0.T, moved_0.T)
+
+    def serve(side, at):
+        cells = cells_buf[at]
+        p_at, q_at = pick(face_parts.at[side], hot_y_of(cells), cells & (CZ - 1))
+        answer[side, 0:1] = p_at
+        answer[side, 1:2] = q_at
+
+    @pl.when(near_up)
+    def _():
+        ask["xd"].wait_recv()
+        serve(1, 2)
+        reply["xu"].start()
+
+    @pl.when(near_down)
+    def _():
+        ask["xu"].wait_recv()
+        serve(0, 1)
+        reply["xd"].start()
+
+    pl.when(near_up)(q_x["xu"].start)
+    pl.when(near_down)(q_x["xd"].start)
+
+    on_face = [
+        pick(slot_parts.at[side], where_hot[side * (CX - 1) * CY:(side * (CX - 1) + 1) * CY], own_z)
+        for side in range(2)
+    ]
 
     def slots_of(k, _):
         pltpu.make_async_copy(slots.at[k], slots.at[k], slot_recv.at[k]).wait()
         prepare(k)
         return 0
 
-    lax.fori_loop(1, NA, slots_of, 0)
+    lax.fori_loop(1, BATCHES[1], slots_of, 0)
     rest = slots.at[pl.ds(1, NA - 1)]
 
-    phase = jnp.cos(0.5 * jnp.full((1, CZ), lax.rem(step_ref[0], 97).astype(F32), F32))
-    for copy in loads[3:]:
-        copy.wait()
-    for faces in (q_x, q_y, p_x, p_y, pq_z):
-        arrive(faces)
+    arrive(pq_z)
     edge_t = jnp.concatenate([zrecv[...], jnp.zeros((CZ - 16, CZ), F32)], axis=0).T
     at_z = lax.broadcasted_iota(jnp.int32, (CY, CZ), 1)
 
@@ -268,40 +360,73 @@
         lower = jnp.where(at_z == 0, low, pltpu.roll(field, 1, 1))
         return (upper - lower) * 0.5
 
-    def slopes(ref, x, at):
-        mid = ref[x + 1, rows_of]
-        return (
-            (ref[x + 2, rows_of] - ref[x, rows_of]) * 0.5,
-            (ref[x + 1, pl.ds(9, CY)] - ref[x + 1, pl.ds(7, CY)]) * 0.5,
-            along_z(mid, edge_t[:, at + x:at + x + 1], edge_t[:, 8 + at + x:8 + at + x + 1]),
-        )
-
     for x in range(CX):
-        dp = slopes(pp, x, 0)
-        dq = slopes(qq, x, CX)
-        free = 1.0 - mask[x].astype(F32)
-        total = [avel[k, x] + dq[k] for k in range(3)]
-        lam0[x + 1] = free * total[0]
-        lam1[x, rows_of] = free * total[1]
-        lam2[x] = free * total[2]
-        sens = -(
-            total[0] * (vel[0, x] - 0.3 * dp[0] + drv[x] * phase)
-            + total[1] * (vel[1, x] - 0.3 * dp[1])
-            + total[2] * (vel[2, x] - 0.3 * dp[2])
-        )
+        dp = along_z(pp[x, rows_of], edge_t[:, x:x + 1], edge_t[:, 8 + x:9 + x])
+        dq = along_z(qq[x, rows_of], edge_t[:, CX + x:CX + x + 1], edge_t[:, 8 + CX + x:9 + CX + x])
+        total_2 = total[2, x] + dq
+        total[2, x] = total_2
+        sens = -(sums[x] + total_2 * (vel[2, x] - 0.3 * dp))
         for i, piece in enumerate(pieces(sens.T)):
             sens_t[i * CZ:(i + 1) * CZ, x * CY:(x + 1) * CY] = piece
 
     picked = jnp.dot(sens_t[...], where_hot[...], preferred_element_type=F32)
     picked = picked[0:CZ] + picked[CZ:2 * CZ] + picked[2 * CZ:3 * CZ]
-    z_at = lax.broadcasted_iota(jnp.int32, (CZ, WALL), 0)
-    vals[0] = jnp.sum(jnp.where(z_at == own_z, picked, 0.0), axis=0, keepdims=True)
+    picked = jnp.sum(jnp.where(y_at == own_z, picked, 0.0), axis=0, keepdims=True)
+
+    pl.when(near_down)(reply["xu"].wait_recv)
+    pl.when(near_up)(reply["xd"].wait_recv)
+
+    def own_answer(side):
+        split_into(wrap_parts, turned_wrap[0], turned_wrap[1])
+        p_at, q_at = pick(wrap_parts, hot_y_of(cells_buf[0]), cells_buf[0] & (CZ - 1))
+        answered[side, 0:1] = p_at
+        answered[side, 1:2] = q_at
+
+    @pl.when(wrap_down)
+    def _():
+        wrap["xu"].wait_recv()
+        own_answer(0)
+
+    @pl.when(wrap_up)
+    def _():
+        wrap["xd"].wait_recv()
+        own_answer(1)
+
+    for side, (total_at, moved_at) in enumerate(on_face):
+        sign = 2.0 * side - 1.0
+        here = own_x == side * (CX - 1)
+        more_total = jnp.where(here, answered[side, 1:2], 0.0) * (0.5 * sign)
+        more_moved = jnp.where(here, answered[side, 0:1], 0.0) * (-0.15 * sign)
+        picked = picked - (more_total * (moved_at + more_moved) + total_at * more_moved)
+    vals[0] = picked
 
     for k in range(NA - 1, 0, -1):
         pltpu.make_async_remote_copy(
             src_ref=vals.at[0], dst_ref=vals.at[k], send_sem=val_send, recv_sem=val_recv.at[k],
             device_id=plane_peer(k), device_id_type=MESH,
         ).start()
+
+    pl.when(near_down)(q_x["xu"].wait_recv)
+    pl.when(near_up)(q_x["xd"].wait_recv)
+
+    @pl.when(wrap_down)
+    def _():
+        q_near[0] = turned_wrap[1].T
+
+    @pl.when(wrap_up)
+    def _():
+        q_near[1] = turned_wrap[1].T
+
+    for x in range(CX):
+        free = 1.0 - mask[x].astype(F32)
+        total_0 = total[0, x]
+        if x == 0:
+            total_0 = total_0 - q_near[0] * 0.5
+        if x == CX - 1:
+            total_0 = total_0 + q_near[1] * 0.5
+        lam0[x + 1] = free * total_0
+        lam1[x, rows_of] = free * total[1, x]
+        lam2[x] = free * total[2, x]
 
     start(lam_x)
     start(lam_y)
@@ -318,16 +443,21 @@
     for copy in stores:
         copy.start()
 
-    def product(k):
-        scaled = jnp.concatenate(pieces(weight[k] * vals[k]), axis=0)
-        return lax.dot_general(hot[k], scaled, (((1,), (1,)), ((), ())), preferred_element_type=F32)
-
-    def add_up(k, total):
-        pltpu.make_async_copy(vals.at[k], vals.at[k], val_recv.at[k]).wait()
-        return total + product(k)
+    lax.fori_loop(BATCHES[1], NA, slots_of, 0)
 
     rest_vals = vals.at[pl.ds(1, NA - 1)]
-    summed = lax.fori_loop(1, NA, add_up, product(0))
+    summed = None
+    for low, high in zip(BATCHES[:-1], BATCHES[1:]):
+        for k in range(max(low, 1), high):
+            pltpu.make_async_copy(vals.at[k], vals.at[k], val_recv.at[k]).wait()
+        split = [pieces(weight[k] * vals[k]) for k in range(low, high)]
+        scaled = jnp.concatenate(
+            [jnp.concatenate([one[i] for one in split], axis=1) for i in range(3)], axis=0
+        )
+        product = lax.dot_general(
+            hot[:, low * WALL:high * WALL], scaled, (((1,), (1,)), ((), ())), preferred_element_type=F32
+        )
+        summed = product if summed is None else summed + product
     summed = summed[:, 0:ANG] + summed[:, ANG:2 * ANG] + summed[:, 2 * ANG:3 * ANG]
     dense[...] = jnp.concatenate([summed, jnp.zeros_like(summed)], axis=1).reshape(NB, OWN, 2 * ANG)
 
@@ -358,8 +488,13 @@
     pltpu.make_async_copy(parts, parts, part_recv).wait()
     grad_out[...] = (dense[b] + jnp.sum(parts[...], axis=0))[:, 0:ANG]
 
-    for faces in (q_x, q_y, p_x, p_y, pq_z, lam_x, lam_y, lam_z):
+    for faces in (q_y, p_y, pq_z, lam_x, lam_y, lam_z):
         sent(faces)
+    pl.when(wrap_up)(wrap["xu"].wait_send)
+    pl.when(wrap_down)(wrap["xd"].wait_send)
+    for faces in (ask, reply, q_x):
+        pl.when(near_up)(faces["xu"].wait_send)
+        pl.when(near_down)(faces["xd"].wait_send)
     pltpu.make_async_copy(rest, rest, slot_send).wait()
     pltpu.make_async_copy(rest_vals, rest_vals, val_send).wait()
     pltpu.make_async_copy(parts, parts, part_send).wait()
@@ -407,8 +542,8 @@
             pltpu.VMEM((1, 1, 1, WALL), F32),
             pltpu.SMEM((1, 1, 1), jnp.int32),
             pltpu.SMEM((1,), jnp.int32),
-            pltpu.VMEM((CX + 2, CY + 16, CZ), F32),
-            pltpu.VMEM((CX + 2, CY + 16, CZ), F32),
+            pltpu.VMEM((CX, CY + 16, CZ), F32),
+            pltpu.VMEM((CX, CY + 16, CZ), F32),
             pltpu.VMEM(block, F32),
             pltpu.VMEM(block, F32),
             pltpu.VMEM(block, F32),
@@ -419,19 +554,30 @@
             pltpu.VMEM((CX, CY + 16, CZ), F32),
             pltpu.VMEM(block, F32),
             pltpu.VMEM(block, F32),
+            pltpu.VMEM(block, F32),
+            pltpu.VMEM((2, CY, CZ), F32),
             pltpu.VMEM((16, CY), F32),
             pltpu.VMEM((16, CY), F32),
             pltpu.VMEM((16, CY), F32),
             pltpu.VMEM((16, CY), F32),
+            pltpu.VMEM((2, 2, CZ, CY), F32),
+            pltpu.VMEM((2, CZ, CY), F32),
+            pltpu.VMEM((2, 6 * CZ, CY), BF16),
+            pltpu.VMEM((6 * CZ, CY), BF16),
+            pltpu.VMEM((2, 6 * CZ, CY), BF16),
+            pltpu.VMEM((3, 1, WALL), jnp.int32),
+            pltpu.VMEM((2, 2, WALL), F32),
+            pltpu.VMEM((2, 2, WALL), F32),
             pltpu.VMEM((NA, 2, WALL), F32),
             pltpu.VMEM((NA, 1, WALL), F32),
-            pltpu.VMEM((NA, WIDTH, WALL), BF16),
+            pltpu.VMEM((WIDTH, NA * WALL), BF16),
             pltpu.VMEM((NA, ANG, WALL), F32),
             pltpu.VMEM((CX * CY, WALL), BF16),
             pltpu.VMEM((3 * CZ, CX * CY), BF16),
             pltpu.VMEM((NB, OWN, 2 * ANG), F32),
             pltpu.VMEM((NB - 1, OWN, 2 * ANG), F32),
             dma((5,)), dma((7,)), dma((4,)), dma((10,)), dma((10,)), dma((6,)), dma((6,)),
+            dma((2,)), dma((2,)), dma((2,)), dma((2,)), dma((2,)), dma((2,)),
             dma, dma((NA,)), dma, dma((NA,)), dma, dma,
         ],
         compiler_params=pltpu.CompilerParams(

time: 35 us -> 34.9 us (level)
  no operation moved by 1% of the time
where the time goes in v4:
time: 34.9 us; the launch traced here: 34.8 us
  Pallas kernels  32.9 us (94%)
  between operations  1.93 us (6%)
    pallas_call x1, Pallas kernels, local(): pl.pallas_call(functools.partial(kernel, ns, nr, nc), out_shape=(pltpu.VM...  31.9 us
    pallas_call x1, Pallas kernels, written(): pl.pallas_call(hand3, out_shape=tuple((jax.ShapeDtypeStruct(o.shape, o.dt...  1 us

profile of v4, /device:TPU:1, one launch (start us, length us, event | category | flops | bytes accessed | tf_op | source)
XLA Modules:
  0.0 34.8 jit_solution(14724064019925676100)
XLA Ops:
  1.9 31.9 %shard_map.139 = (f32[4,128,128]{2,1,0:T(8,128)S(1)}, f32[3,4,128,128]{3,2,1,0:T(8,128)S(1)}, f32[8,64]{1,0:T(8,128)S(1)}) custom-call(f32[4,128,128]{2,1,0:T(8,128)} %p_in.1, f32[3,4,128,128]{3,2,1,0:T(8,128)} %v_in.1, f32[4,128,128]{2,1,0:T(8,128)} %kap_in.1, f32[4,128,128]{2,1,0:T(8,128)} %drv_in.1, f32[4,128,128]{2,1,0:T(8,128)} %ap_in.1, ...), custom_call_target="tpu_custom_call" | custom-call | flops 1000000000 | bytes 4000000 | tf_op jit(solution)/shard_map/pallas_call | solution.py:530
  33.8 1.0 %shard_map.140 = (f32[4,128,128]{2,1,0:T(8,128)}, f32[3,4,128,128]{3,2,1,0:T(8,128)}, f32[8,64]{1,0:T(8,128)}) custom-call(f32[4,128,128]{2,1,0:T(8,128)S(1)} %get-tuple-element.6.a, f32[3,4,128,128]{3,2,1,0:T(8,128)S(1)} %get-tuple-element.7.b, f32[8,64]{1,0:T(8,128)S(1)} %get-tuple-element.8.c), custom_call_target="tpu_custom_call" | custom-call | tf_op jit(solution)/shard_map/pallas_call | solution.py:507

commit v5 on v4

--- a/solution.py
+++ b/solution.py
@@ -44,10 +44,11 @@
     ap_out, av_out, grad_out,
     cells_ref, rows_ref, angle_ref, count_ref, step_ref,
     pp, qq, kap, drv, ap, vel, total, mask,
-    lam0, lam1, lam2, apo, sums, q_near,
+    lam0, lam1, lam2, apo, q_near,
     zsend, zrecv, lsend, lrecv,
     turned_face, turned_wrap, face_parts, wrap_parts, slot_parts,
     cells_buf, answer, answered,
+    ends, own_hot_y,
     slots, vals, hot, weight, where_hot, sens_t, dense, parts,
     small_sem, load_sem, store_sem, halo_send, halo_recv, lam_send, lam_recv,
     wrap_send, wrap_recv, cell_send, cell_recv, answer_send, answer_recv,
@@ -208,6 +209,8 @@
     def hot_y_of(cells):
         return jnp.where(y_at == ((cells >> 7) & (CY - 1)), 1.0, 0.0).astype(BF16)
 
+    own_hot_y[...] = hot_y_of(own_cells)
+
     pl.semaphore_wait(barrier, partners)
 
     def slot_copy(k):
@@ -281,13 +284,13 @@
         for side, copy in faces.items():
             pl.when(has[side])(copy.wait_send)
 
+    start(pq_z)
+    start(q_y)
+    start(p_y)
+    pl.when(near_up)(ask["xu"].start)
+    pl.when(near_down)(ask["xd"].start)
     pl.when(wrap_up)(wrap["xu"].start)
     pl.when(wrap_down)(wrap["xd"].start)
-    start(pq_z)
-    pl.when(near_up)(ask["xu"].start)
-    pl.when(near_down)(ask["xd"].start)
-    start(q_y)
-    start(p_y)
     for k in range(NA - 1, 0, -1):
         slot_copy(k).start()
 
@@ -307,15 +310,33 @@
     def along_y(ref, x):
         return (ref[x, pl.ds(9, CY)] - ref[x, pl.ds(7, CY)]) * 0.5
 
+    at_z = lax.broadcasted_iota(jnp.int32, (CY, CZ), 1)
+
+    def along_z(field):
+        upper = jnp.where(at_z == CZ - 1, 0.0, pltpu.roll(field, CZ - 1, 1))
+        lower = jnp.where(at_z == 0, 0.0, pltpu.roll(field, 1, 1))
+        return (upper - lower) * 0.5
+
     for x in range(CX):
+        here = slice(x * CY, (x + 1) * CY)
         total_0 = total[0, x] + along_x(qq, x)
         total_1 = total[1, x] + along_y(qq, x)
+        total_2 = total[2, x] + along_z(qq[x, rows_of])
         total[0, x] = total_0
         total[1, x] = total_1
+        total[2, x] = total_2
         moved_0 = vel[0, x] - 0.3 * along_x(pp, x) + drv[x] * phase
-        sums[x] = total_0 * moved_0 + total_1 * (vel[1, x] - 0.3 * along_y(pp, x))
+        moved_2 = vel[2, x] - 0.3 * along_z(pp[x, rows_of])
+        sens = -(
+            total_0 * moved_0 + total_1 * (vel[1, x] - 0.3 * along_y(pp, x)) + total_2 * moved_2
+        )
+        for i, piece in enumerate(pieces(sens.T)):
+            sens_t[i * CZ:(i + 1) * CZ, here] = piece
         if x in (0, CX - 1):
             split_into(slot_parts.at[x // (CX - 1)], total_0.T, moved_0.T)
+        for i, field in enumerate((total_2.T, moved_2.T)):
+            ends[i:i + 1, here] = field[0:1]
+            ends[2 + i:3 + i, here] = field[CZ - 1:CZ]
 
     def serve(side, at):
         cells = cells_buf[at]
@@ -343,42 +364,38 @@
         for side in range(2)
     ]
 
-    def slots_of(k, _):
-        pltpu.make_async_copy(slots.at[k], slots.at[k], slot_recv.at[k]).wait()
-        prepare(k)
-        return 0
-
-    lax.fori_loop(1, BATCHES[1], slots_of, 0)
-    rest = slots.at[pl.ds(1, NA - 1)]
-
-    arrive(pq_z)
-    edge_t = jnp.concatenate([zrecv[...], jnp.zeros((CZ - 16, CZ), F32)], axis=0).T
-    at_z = lax.broadcasted_iota(jnp.int32, (CY, CZ), 1)
-
-    def along_z(field, low, high):
-        upper = jnp.where(at_z == CZ - 1, high, pltpu.roll(field, CZ - 1, 1))
-        lower = jnp.where(at_z == 0, low, pltpu.roll(field, 1, 1))
-        return (upper - lower) * 0.5
-
-    for x in range(CX):
-        dp = along_z(pp[x, rows_of], edge_t[:, x:x + 1], edge_t[:, 8 + x:9 + x])
-        dq = along_z(qq[x, rows_of], edge_t[:, CX + x:CX + x + 1], edge_t[:, 8 + CX + x:9 + CX + x])
-        total_2 = total[2, x] + dq
-        total[2, x] = total_2
-        sens = -(sums[x] + total_2 * (vel[2, x] - 0.3 * dp))
-        for i, piece in enumerate(pieces(sens.T)):
-            sens_t[i * CZ:(i + 1) * CZ, x * CY:(x + 1) * CY] = piece
+    edge_parts = jnp.concatenate(pieces(ends[...]), axis=0)
+    edge = jnp.dot(edge_parts, where_hot[...], preferred_element_type=F32)
+    edge = edge[0:4] + edge[4:8] + edge[8:12]
 
     picked = jnp.dot(sens_t[...], where_hot[...], preferred_element_type=F32)
     picked = picked[0:CZ] + picked[CZ:2 * CZ] + picked[2 * CZ:3 * CZ]
     picked = jnp.sum(jnp.where(y_at == own_z, picked, 0.0), axis=0, keepdims=True)
 
+    def corrected(value, side, here, total_at, moved_at, p_at, q_at):
+        sign = 2.0 * side - 1.0
+        more_total = jnp.where(here, q_at, 0.0) * (0.5 * sign)
+        more_moved = jnp.where(here, p_at, 0.0) * (-0.15 * sign)
+        return value - (more_total * (moved_at + more_moved) + total_at * more_moved)
+
+    arrive(pq_z)
+    z_parts = jnp.concatenate(pieces(zrecv[...]), axis=0)
+    faces_z = jnp.dot(z_parts, own_hot_y[...], preferred_element_type=F32)
+    faces_z = faces_z[0:16] + faces_z[16:32] + faces_z[32:48]
+    row_x = lax.broadcasted_iota(jnp.int32, (16, WALL), 0) & (CX - 1)
+    faces_z = jnp.where(row_x == own_x, faces_z, 0.0)
+    for side in range(2):
+        p_at = jnp.sum(faces_z[8 * side:8 * side + 4], axis=0, keepdims=True)
+        q_at = jnp.sum(faces_z[8 * side + 4:8 * side + 8], axis=0, keepdims=True)
+        here = own_z == side * (CZ - 1)
+        picked = corrected(picked, side, here, edge[2 * side:2 * side + 1], edge[2 * side + 1:2 * side + 2], p_at, q_at)
+
     pl.when(near_down)(reply["xu"].wait_recv)
     pl.when(near_up)(reply["xd"].wait_recv)
 
     def own_answer(side):
         split_into(wrap_parts, turned_wrap[0], turned_wrap[1])
-        p_at, q_at = pick(wrap_parts, hot_y_of(cells_buf[0]), cells_buf[0] & (CZ - 1))
+        p_at, q_at = pick(wrap_parts, own_hot_y[...], cells_buf[0] & (CZ - 1))
         answered[side, 0:1] = p_at
         answered[side, 1:2] = q_at
 
@@ -393,11 +410,8 @@
         own_answer(1)
 
     for side, (total_at, moved_at) in enumerate(on_face):
-        sign = 2.0 * side - 1.0
         here = own_x == side * (CX - 1)
-        more_total = jnp.where(here, answered[side, 1:2], 0.0) * (0.5 * sign)
-        more_moved = jnp.where(here, answered[side, 0:1], 0.0) * (-0.15 * sign)
-        picked = picked - (more_total * (moved_at + more_moved) + total_at * more_moved)
+        picked = corrected(picked, side, here, total_at, moved_at, answered[side, 0:1], answered[side, 1:2])
     vals[0] = picked
 
     for k in range(NA - 1, 0, -1):
@@ -416,6 +430,12 @@
     @pl.when(wrap_up)
     def _():
         q_near[1] = turned_wrap[1].T
+
+    edge_t = jnp.concatenate([zrecv[...], jnp.zeros((CZ - 16, CZ), F32)], axis=0).T
+
+    def with_edges(field, low, high):
+        field = jnp.where(at_z == CZ - 1, field + high * 0.5, field)
+        return jnp.where(at_z == 0, field - low * 0.5, field)
 
     for x in range(CX):
         free = 1.0 - mask[x].astype(F32)
@@ -426,7 +446,8 @@
             total_0 = total_0 + q_near[1] * 0.5
         lam0[x + 1] = free * total_0
         lam1[x, rows_of] = free * total[1, x]
-        lam2[x] = free * total[2, x]
+        low, high = (edge_t[:, 8 * i + CX + x:8 * i + CX + x + 1] for i in range(2))
+        lam2[x] = free * with_edges(total[2, x], low, high)
 
     start(lam_x)
     start(lam_y)
@@ -443,7 +464,13 @@
     for copy in stores:
         copy.start()
 
-    lax.fori_loop(BATCHES[1], NA, slots_of, 0)
+    def slots_of(k, _):
+        pltpu.make_async_copy(slots.at[k], slots.at[k], slot_recv.at[k]).wait()
+        prepare(k)
+        return 0
+
+    rest = slots.at[pl.ds(1, NA - 1)]
+    lax.fori_loop(1, NA, slots_of, 0)
 
     rest_vals = vals.at[pl.ds(1, NA - 1)]
     summed = None
@@ -479,7 +506,7 @@
         div = (
             (lam0[x + 2] - lam0[x]) * 0.5
             + (lam1[x, pl.ds(9, CY)] - lam1[x, pl.ds(7, CY)]) * 0.5
-            + along_z(lam2[x], edge_l[:, x:x + 1], edge_l[:, 8 + x:9 + x])
+            + with_edges(along_z(lam2[x]), edge_l[:, x:x + 1], edge_l[:, 8 + x:9 + x])
         )
         apo[x] = ap[x] + 0.3 * div
     last = pltpu.make_async_copy(apo, ap_out, store_sem.at[3])
@@ -554,7 +581,6 @@
             pltpu.VMEM((CX, CY + 16, CZ), F32),
             pltpu.VMEM(block, F32),
             pltpu.VMEM(block, F32),
-            pltpu.VMEM(block, F32),
             pltpu.VMEM((2, CY, CZ), F32),
             pltpu.VMEM((16, CY), F32),
             pltpu.VMEM((16, CY), F32),
@@ -568,6 +594,8 @@
             pltpu.VMEM((3, 1, WALL), jnp.int32),
             pltpu.VMEM((2, 2, WALL), F32),
             pltpu.VMEM((2, 2, WALL), F32),
+            pltpu.VMEM((4, CX * CY), F32),
+            pltpu.VMEM((CY, WALL), BF16),
             pltpu.VMEM((NA, 2, WALL), F32),
             pltpu.VMEM((NA, 1, WALL), F32),
             pltpu.VMEM((WIDTH, NA * WALL), BF16),

time: 34.9 us -> 32.8 us (0.940)
  Pallas kernels: 32.9 us -> 30.8 us
    pallas_call x1, Pallas kernels: 31.9 us -> 29.8 us  [local(): pl.pallas_call(functools.partial(kernel, ns, nr, nc), out_shape=(pltpu.VM...]
where the time goes in v5:
time: 32.8 us; the launch traced here: 32.7 us
  Pallas kernels  30.8 us (94%)
  between operations  1.93 us (6%)
    pallas_call x1, Pallas kernels, local(): pl.pallas_call(functools.partial(kernel, ns, nr, nc), out_shape=(pltpu.VM...  29.8 us
    pallas_call x1, Pallas kernels, written(): pl.pallas_call(hand3, out_shape=tuple((jax.ShapeDtypeStruct(o.shape, o.dt...  1 us

profile of v5, /device:TPU:1, one launch (start us, length us, event | category | flops | bytes accessed | tf_op | source)
XLA Modules:
  0.0 32.7 jit_solution(11730389072970594805)
XLA Ops:
  1.9 29.8 %shard_map.139 = (f32[4,128,128]{2,1,0:T(8,128)S(1)}, f32[3,4,128,128]{3,2,1,0:T(8,128)S(1)}, f32[8,64]{1,0:T(8,128)S(1)}) custom-call(f32[4,128,128]{2,1,0:T(8,128)} %p_in.1, f32[3,4,128,128]{3,2,1,0:T(8,128)} %v_in.1, f32[4,128,128]{2,1,0:T(8,128)} %kap_in.1, f32[4,128,128]{2,1,0:T(8,128)} %drv_in.1, f32[4,128,128]{2,1,0:T(8,128)} %ap_in.1, ...), custom_call_target="tpu_custom_call" | custom-call | flops 1000000000 | bytes 4000000 | tf_op jit(solution)/shard_map/pallas_call | solution.py:557
  31.7 1.0 %shard_map.140 = (f32[4,128,128]{2,1,0:T(8,128)}, f32[3,4,128,128]{3,2,1,0:T(8,128)}, f32[8,64]{1,0:T(8,128)}) custom-call(f32[4,128,128]{2,1,0:T(8,128)S(1)} %get-tuple-element.6.a, f32[3,4,128,128]{3,2,1,0:T(8,128)S(1)} %get-tuple-element.7.b, f32[8,64]{1,0:T(8,128)S(1)} %get-tuple-element.8.c), custom_call_target="tpu_custom_call" | custom-call | tf_op jit(solution)/shard_map/pallas_call | solution.py:534

commit v6 on v5

--- a/solution.py
+++ b/solution.py
@@ -72,6 +72,54 @@
         other_zh = lax.rem(zh + lax.rem(k, ZH), ZH)
         return (y * ZL + other_zl, other_r, x_at * ZH + other_zh)
 
+    plane = jnp.zeros((CY, CZ), F32)
+    strip = jnp.zeros((8, CZ), F32)
+    for ref in (pp, qq, lam1):
+        for x in range(CX):
+            ref[x, pl.ds(0, 8)] = strip
+            ref[x, pl.ds(CY + 8, 8)] = strip
+    for ref in (q_near, ):
+        ref[0] = plane
+        ref[1] = plane
+    lam0[0] = plane
+    lam0[CX + 1] = plane
+    zrecv[...] = jnp.zeros_like(zrecv)
+    lrecv[...] = jnp.zeros_like(lrecv)
+    answered[...] = jnp.zeros_like(answered)
+
+    barrier = pltpu.get_barrier_semaphore()
+
+    def greet(device):
+        pl.semaphore_signal(barrier, inc=1, device_id=device, device_id_type=MESH)
+
+    def greet_line(k, _):
+        greet(line_peer(k))
+        return 0
+
+    s_up, s_down = jnp.minimum(s + 1, ns - 1), jnp.maximum(s - 1, 0)
+    r_up, r_down = jnp.minimum(r + 1, nr - 1), jnp.maximum(r - 1, 0)
+    c_up, c_down = jnp.minimum(c + 1, nc - 1), jnp.maximum(c - 1, 0)
+    has = {
+        "xu": s < ns - 1, "xd": s > 0, "yu": r < nr - 1, "yd": r > 0, "zu": c < nc - 1, "zd": c > 0,
+    }
+    wrap_up = jnp.logical_and(zl == ZL - 1, has["xu"])
+    wrap_down = jnp.logical_and(zl == 0, has["xd"])
+    near_up = zl < ZL - 1
+    near_down = zl > 0
+    beyond = (
+        (jnp.logical_and(zh == ZH - 1, has["zu"]), (s, r, c_up)),
+        (jnp.logical_and(zh == 0, has["zd"]), (s, r, c_down)),
+        (wrap_up, (s_up, r, c)),
+        (wrap_down, (s_down, r, c)),
+    )
+    partners = NA - 1 + NB - 1
+    for here, device in beyond:
+        pl.when(here)(functools.partial(greet, device))
+        partners = partners + here.astype(jnp.int32)
+    for k in range(1, NA):
+        greet(plane_peer(k))
+    lax.fori_loop(1, NB, greet_line, 0)
+
     loads = [
         pltpu.make_async_copy(kap_in, kap, load_sem.at[0]),
         pltpu.make_async_copy(ap_in, ap, load_sem.at[1]),
@@ -91,54 +139,6 @@
     for copy in small + loads:
         copy.start()
 
-    plane = jnp.zeros((CY, CZ), F32)
-    strip = jnp.zeros((8, CZ), F32)
-    for ref in (pp, qq, lam1):
-        for x in range(CX):
-            ref[x, pl.ds(0, 8)] = strip
-            ref[x, pl.ds(CY + 8, 8)] = strip
-    for ref in (q_near, ):
-        ref[0] = plane
-        ref[1] = plane
-    lam0[0] = plane
-    lam0[CX + 1] = plane
-    zrecv[...] = jnp.zeros_like(zrecv)
-    lrecv[...] = jnp.zeros_like(lrecv)
-    answered[...] = jnp.zeros_like(answered)
-
-    barrier = pltpu.get_barrier_semaphore()
-
-    def greet(device):
-        pl.semaphore_signal(barrier, inc=1, device_id=device, device_id_type=MESH)
-
-    def greet_line(k, _):
-        greet(line_peer(k))
-        return 0
-
-    s_up, s_down = jnp.minimum(s + 1, ns - 1), jnp.maximum(s - 1, 0)
-    r_up, r_down = jnp.minimum(r + 1, nr - 1), jnp.maximum(r - 1, 0)
-    c_up, c_down = jnp.minimum(c + 1, nc - 1), jnp.maximum(c - 1, 0)
-    has = {
-        "xu": s < ns - 1, "xd": s > 0, "yu": r < nr - 1, "yd": r > 0, "zu": c < nc - 1, "zd": c > 0,
-    }
-    wrap_up = jnp.logical_and(zl == ZL - 1, has["xu"])
-    wrap_down = jnp.logical_and(zl == 0, has["xd"])
-    near_up = zl < ZL - 1
-    near_down = zl > 0
-    beyond = (
-        (jnp.logical_and(zh == ZH - 1, has["zu"]), (s, r, c_up)),
-        (jnp.logical_and(zh == 0, has["zd"]), (s, r, c_down)),
-        (wrap_up, (s_up, r, c)),
-        (wrap_down, (s_down, r, c)),
-    )
-    partners = NA - 1 + NB - 1
-    for here, device in beyond:
-        pl.when(here)(functools.partial(greet, device))
-        partners = partners + here.astype(jnp.int32)
-    for k in range(1, NA):
-        greet(plane_peer(k))
-    lax.fori_loop(1, NB, greet_line, 0)
-
     lane = lax.broadcasted_iota(jnp.int32, (1, WALL), 1)
     for copy in small:
         copy.wait()
@@ -164,16 +164,12 @@
         near = jnp.maximum(1.0 - dist, 0.0)
         weight[k] = (outer * outer * outer - 4.0 * near * near * near) * (1.0 / 6.0)
 
-    prepare(0)
 
     own_cells = cells_ref[0, 0]
     cells_buf[0] = own_cells
     own_xy = own_cells >> 7
     own_x = own_cells >> 14
     own_z = own_cells & (CZ - 1)
-    y_at = lax.broadcasted_iota(jnp.int32, (CY, WALL), 0)
-    for x in range(CX):
-        where_hot[x * CY:(x + 1) * CY] = jnp.where(y_at + x * CY == own_xy, 1.0, 0.0).astype(BF16)
 
     loads[0].wait()
     loads[1].wait()
@@ -194,9 +190,6 @@
             for j, piece in enumerate(pieces(field)):
                 ref[(3 * i + j) * CZ:(3 * i + j + 1) * CZ] = piece
 
-    for side in range(2):
-        split_into(face_parts.at[side], turned_face[side, 0], turned_face[side, 1])
-
     def pick(ref, hot_y, at_z):
         got = jnp.dot(ref[...], hot_y, preferred_element_type=F32)
         out = []
@@ -209,7 +202,6 @@
     def hot_y_of(cells):
         return jnp.where(y_at == ((cells >> 7) & (CY - 1)), 1.0, 0.0).astype(BF16)
 
-    own_hot_y[...] = hot_y_of(own_cells)
 
     pl.semaphore_wait(barrier, partners)
 
@@ -293,6 +285,14 @@
     pl.when(wrap_down)(wrap["xd"].start)
     for k in range(NA - 1, 0, -1):
         slot_copy(k).start()
+
+    y_at = lax.broadcasted_iota(jnp.int32, (CY, WALL), 0)
+    for x in range(CX):
+        where_hot[x * CY:(x + 1) * CY] = jnp.where(y_at + x * CY == own_xy, 1.0, 0.0).astype(BF16)
+    own_hot_y[...] = hot_y_of(own_cells)
+    for side in range(2):
+        split_into(face_parts.at[side], turned_face[side, 0], turned_face[side, 1])
+    prepare(0)
 
     phase = jnp.cos(0.5 * jnp.full((1, CZ), lax.rem(step_ref[0], 97).astype(F32), F32))
     for copy in loads[3:]:
@@ -532,17 +532,23 @@
 def written(outs):
     anyspace = pl.BlockSpec(memory_space=pl.ANY)
     return pl.pallas_call(
-        hand3,
+        hand_over,
         out_shape=tuple(jax.ShapeDtypeStruct(o.shape, o.dtype) for o in outs),
         in_specs=[anyspace] * 3,
         out_specs=(anyspace,) * 3,
-        scratch_shapes=[pltpu.SemaphoreType.DMA((3,))],
+        scratch_shapes=[pltpu.SemaphoreType.DMA((9,))],
         compiler_params=pltpu.CompilerParams(vmem_limit_bytes=1024 * 1024),
     )(*outs)
 
 
-def hand3(a, b, c, d, e, f, sem):
-    copies = [pltpu.make_async_copy(x, y, sem.at[i]) for i, (x, y) in enumerate(((a, d), (b, e), (c, f)))]
+def hand_over(adj_p, adj_v, grad, adj_p_out, adj_v_out, grad_out, sem):
+    pairs = [(grad, grad_out)]
+    for x in range(0, CX, 2):
+        here = pl.ds(x, 2)
+        pairs.append((adj_p.at[here], adj_p_out.at[here]))
+        for k in range(3):
+            pairs.append((adj_v.at[k, here], adj_v_out.at[k, here]))
+    copies = [pltpu.make_async_copy(a, b, sem.at[i]) for i, (a, b) in enumerate(pairs)]
     for copy in copies:
         copy.start()
     for copy in copies:

time: 32.8 us -> 32.9 us (level)
  no operation moved by 1% of the time
where the time goes in v6:
time: 32.9 us; the launch traced here: 32.8 us
  Pallas kernels  30.9 us (94%)
  between operations  1.93 us (6%)
    pallas_call x1, Pallas kernels, local(): pl.pallas_call(functools.partial(kernel, ns, nr, nc), out_shape=(pltpu.VM...  29.8 us
    pallas_call x1, Pallas kernels, written(): pl.pallas_call(hand_over, out_shape=tuple((jax.ShapeDtypeStruct(o.shape,...  1.04 us

profile of v6, /device:TPU:1, one launch (start us, length us, event | category | flops | bytes accessed | tf_op | source)
XLA Modules:
  0.0 32.8 jit_solution(13469518380658826454)
XLA Ops:
  1.9 29.8 %shard_map.139 = (f32[4,128,128]{2,1,0:T(8,128)S(1)}, f32[3,4,128,128]{3,2,1,0:T(8,128)S(1)}, f32[8,64]{1,0:T(8,128)S(1)}) custom-call(f32[4,128,128]{2,1,0:T(8,128)} %p_in.1, f32[3,4,128,128]{3,2,1,0:T(8,128)} %v_in.1, f32[4,128,128]{2,1,0:T(8,128)} %kap_in.1, f32[4,128,128]{2,1,0:T(8,128)} %drv_in.1, f32[4,128,128]{2,1,0:T(8,128)} %ap_in.1, ...), custom_call_target="tpu_custom_call" | custom-call | flops 1000000000 | bytes 4000000 | tf_op jit(solution)/shard_map/pallas_call | solution.py:563
  31.7 1.0 %shard_map.140 = (f32[4,128,128]{2,1,0:T(8,128)}, f32[3,4,128,128]{3,2,1,0:T(8,128)}, f32[8,64]{1,0:T(8,128)}) custom-call(f32[4,128,128]{2,1,0:T(8,128)S(1)} %get-tuple-element.6.adj_p, f32[3,4,128,128]{3,2,1,0:T(8,128)S(1)} %get-tuple-element.7.adj_v, f32[8,64]{1,0:T(8,128)S(1)} %get-tuple-element.8.grad), custom_call_target="tpu_custom_call" | custom-call | tf_op jit(solution)/shard_map/pallas_call | solution.py:534

commit v7 on v6

--- a/solution.py
+++ b/solution.py
@@ -21,6 +21,7 @@
 NB = 2 * ZL * ZH
 WIDTH = NB * OWN
 BATCHES = (0, 5, 11, 16)
+LINE = sorted(range(1, 16), key=lambda k: (-(k & 1), abs((k >> 2) - 2), k))
 MESH = pl.DeviceIdType.MESH
 PLANE = sorted(
     ((dy, dx) for dy in range(NYC) for dx in range(NXC)),
@@ -57,19 +58,20 @@
     s = lax.axis_index("slab")
     r = lax.axis_index("row")
     c = lax.axis_index("col")
-    y, zl = lax.div(s, ZL), lax.rem(s, ZL)
-    x_at, zh = lax.div(c, ZH), lax.rem(c, ZH)
+    y, zl = s >> 2, s & (ZL - 1)
+    x_at, zh = c >> 1, c & (ZH - 1)
     group = y * NXC + x_at
     b = (zl * 2 + r) * ZH + zh
 
     def plane_peer(k):
         dy, dx = PLANE[k]
-        return (lax.rem(y + dy, NYC) * ZL + zl, r, lax.rem(x_at + dx, NXC) * ZH + zh)
+        return (((y + dy) & (NYC - 1)) * ZL + zl, r, ((x_at + dx) & (NXC - 1)) * ZH + zh)
+
+    def line_place(k):
+        return (zl + (k >> 2)) & (ZL - 1), r ^ ((k >> 1) & 1), zh ^ (k & 1)
 
     def line_peer(k):
-        other_zl = lax.rem(zl + lax.div(k, 2 * ZH), ZL)
-        other_r = lax.rem(r + lax.rem(lax.div(k, ZH), 2), 2)
-        other_zh = lax.rem(zh + lax.rem(k, ZH), ZH)
+        other_zl, other_r, other_zh = line_place(k)
         return (y * ZL + other_zl, other_r, x_at * ZH + other_zh)
 
     plane = jnp.zeros((CY, CZ), F32)
@@ -92,10 +94,6 @@
     def greet(device):
         pl.semaphore_signal(barrier, inc=1, device_id=device, device_id_type=MESH)
 
-    def greet_line(k, _):
-        greet(line_peer(k))
-        return 0
-
     s_up, s_down = jnp.minimum(s + 1, ns - 1), jnp.maximum(s - 1, 0)
     r_up, r_down = jnp.minimum(r + 1, nr - 1), jnp.maximum(r - 1, 0)
     c_up, c_down = jnp.minimum(c + 1, nc - 1), jnp.maximum(c - 1, 0)
@@ -116,9 +114,10 @@
     for here, device in beyond:
         pl.when(here)(functools.partial(greet, device))
         partners = partners + here.astype(jnp.int32)
-    for k in range(1, NA):
+    for k in range(NA - 1, 0, -1):
         greet(plane_peer(k))
-    lax.fori_loop(1, NB, greet_line, 0)
+    for k in LINE:
+        greet(line_peer(k))
 
     loads = [
         pltpu.make_async_copy(kap_in, kap, load_sem.at[0]),
@@ -147,7 +146,8 @@
     bits = own_rows >> 3
     owner_group = ((bits >> 6) << 2) + ((bits >> 1) & 3)
     owner_line = (((bits >> 4) & 3) << 2) + (((bits >> 3) & 1) << 1) + (bits & 1)
-    code = owner_group * WIDTH + owner_line * OWN + (own_rows & (OWN - 1))
+    half = (own_rows >> 2) & 1
+    code = owner_group * WIDTH + half * (WIDTH // 2) + owner_line * (OWN // 2) + (own_rows & (OWN // 2 - 1))
     slots[0, 0:1] = jnp.where(live, code.astype(F32), -1.0)
     slots[0, 1:2] = angle_ref[0, 0]
     row_at = (lax.broadcasted_iota(jnp.int32, (WIDTH, WALL), 0) + group * WIDTH).astype(F32)
@@ -486,18 +486,15 @@
         )
         summed = product if summed is None else summed + product
     summed = summed[:, 0:ANG] + summed[:, ANG:2 * ANG] + summed[:, 2 * ANG:3 * ANG]
-    dense[...] = jnp.concatenate([summed, jnp.zeros_like(summed)], axis=1).reshape(NB, OWN, 2 * ANG)
-
-    def send_part(k, _):
-        peer = line_peer(k)
-        other = (lax.rem(peer[0], ZL) * 2 + peer[1]) * ZH + lax.rem(peer[2], ZH)
+    packed = jnp.concatenate([summed[0:WIDTH // 2], summed[WIDTH // 2:WIDTH]], axis=1)
+    dense[...] = packed.reshape(NB, OWN // 2, 2 * ANG)
+
+    for k in LINE:
+        other_zl, other_r, other_zh = line_place(k)
         pltpu.make_async_remote_copy(
-            src_ref=dense.at[other], dst_ref=parts.at[k - 1], send_sem=part_send, recv_sem=part_recv,
-            device_id=peer, device_id_type=MESH,
+            src_ref=dense.at[(other_zl * 2 + other_r) * ZH + other_zh], dst_ref=parts.at[k - 1],
+            send_sem=part_send, recv_sem=part_recv, device_id=line_peer(k), device_id_type=MESH,
         ).start()
-        return 0
-
-    lax.fori_loop(1, NB, send_part, 0)
 
     for faces in (lam_x, lam_y, lam_z):
         arrive(faces)
@@ -513,7 +510,8 @@
     last.start()
 
     pltpu.make_async_copy(parts, parts, part_recv).wait()
-    grad_out[...] = (dense[b] + jnp.sum(parts[...], axis=0))[:, 0:ANG]
+    own = dense[b] + jnp.sum(parts[...], axis=0)
+    grad_out[...] = jnp.concatenate([own[:, 0:ANG], own[:, ANG:2 * ANG]], axis=0)
 
     for faces in (q_y, p_y, pq_z, lam_x, lam_y, lam_z):
         sent(faces)
@@ -608,8 +606,8 @@
             pltpu.VMEM((NA, ANG, WALL), F32),
             pltpu.VMEM((CX * CY, WALL), BF16),
             pltpu.VMEM((3 * CZ, CX * CY), BF16),
-            pltpu.VMEM((NB, OWN, 2 * ANG), F32),
-            pltpu.VMEM((NB - 1, OWN, 2 * ANG), F32),
+            pltpu.VMEM((NB, OWN // 2, 2 * ANG), F32),
+            pltpu.VMEM((NB - 1, OWN // 2, 2 * ANG), F32),
             dma((5,)), dma((7,)), dma((4,)), dma((10,)), dma((10,)), dma((6,)), dma((6,)),
             dma((2,)), dma((2,)), dma((2,)), dma((2,)), dma((2,)), dma((2,)),
             dma, dma((NA,)), dma, dma((NA,)), dma, dma,

time: 32.9 us -> 32.1 us (0.976)
  Pallas kernels: 30.9 us -> 30.1 us
    pallas_call x1, Pallas kernels: 29.8 us -> 29 us  [local(): pl.pallas_call(functools.partial(kernel, ns, nr, nc), out_shape=(pltpu.VM...]
where the time goes in v7:
time: 32.1 us; the launch traced here: 32 us
  Pallas kernels  30.1 us (94%)
  between operations  1.93 us (6%)
    pallas_call x1, Pallas kernels, local(): pl.pallas_call(functools.partial(kernel, ns, nr, nc), out_shape=(pltpu.VM...  29 us
    pallas_call x1, Pallas kernels, written(): pl.pallas_call(hand_over, out_shape=tuple((jax.ShapeDtypeStruct(o.shape,...  1.04 us

profile of v7, /device:TPU:1, one launch (start us, length us, event | category | flops | bytes accessed | tf_op | source)
XLA Modules:
  0.0 32.0 jit_solution(634127428257690681)
XLA Ops:
  1.9 29.0 %shard_map.139 = (f32[4,128,128]{2,1,0:T(8,128)S(1)}, f32[3,4,128,128]{3,2,1,0:T(8,128)S(1)}, f32[8,64]{1,0:T(8,128)S(1)}) custom-call(f32[4,128,128]{2,1,0:T(8,128)} %p_in.1, f32[3,4,128,128]{3,2,1,0:T(8,128)} %v_in.1, f32[4,128,128]{2,1,0:T(8,128)} %kap_in.1, f32[4,128,128]{2,1,0:T(8,128)} %drv_in.1, f32[4,128,128]{2,1,0:T(8,128)} %ap_in.1, ...), custom_call_target="tpu_custom_call" | custom-call | flops 1000000000 | bytes 4000000 | tf_op jit(solution)/shard_map/pallas_call | solution.py:561
  31.0 1.0 %shard_map.140 = (f32[4,128,128]{2,1,0:T(8,128)}, f32[3,4,128,128]{3,2,1,0:T(8,128)}, f32[8,64]{1,0:T(8,128)}) custom-call(f32[4,128,128]{2,1,0:T(8,128)S(1)} %get-tuple-element.6.adj_p, f32[3,4,128,128]{3,2,1,0:T(8,128)S(1)} %get-tuple-element.7.adj_v, f32[8,64]{1,0:T(8,128)S(1)} %get-tuple-element.8.grad), custom_call_target="tpu_custom_call" | custom-call | tf_op jit(solution)/shard_map/pallas_call | solution.py:532

commit v8 on v7

--- a/solution.py
+++ b/solution.py
@@ -185,17 +185,20 @@
             if x in (0, CX - 1):
                 turned_face[x // (CX - 1), i] = turned
 
+    picks = 2
+
     def split_into(ref, first, second):
         for i, field in enumerate((first, second)):
-            for j, piece in enumerate(pieces(field)):
-                ref[(3 * i + j) * CZ:(3 * i + j + 1) * CZ] = piece
+            for j, piece in enumerate(pieces(field)[:picks]):
+                ref[(picks * i + j) * CZ:(picks * i + j + 1) * CZ] = piece
 
     def pick(ref, hot_y, at_z):
-        got = jnp.dot(ref[...], hot_y, preferred_element_type=F32)
+        got = jnp.dot(ref[0:2 * picks * CZ], hot_y, preferred_element_type=F32)
         out = []
         for i in range(2):
-            field = got[3 * i * CZ:(3 * i + 1) * CZ]
-            field = field + got[(3 * i + 1) * CZ:(3 * i + 2) * CZ] + got[(3 * i + 2) * CZ:(3 * i + 3) * CZ]
+            field = got[picks * i * CZ:(picks * i + 1) * CZ]
+            for j in range(1, picks):
+                field = field + got[(picks * i + j) * CZ:(picks * i + j + 1) * CZ]
             out.append(jnp.sum(jnp.where(y_at == at_z, field, 0.0), axis=0, keepdims=True))
         return out
 
@@ -477,15 +480,15 @@
     for low, high in zip(BATCHES[:-1], BATCHES[1:]):
         for k in range(max(low, 1), high):
             pltpu.make_async_copy(vals.at[k], vals.at[k], val_recv.at[k]).wait()
-        split = [pieces(weight[k] * vals[k]) for k in range(low, high)]
+        split = [pieces(weight[k] * vals[k])[:2] for k in range(low, high)]
         scaled = jnp.concatenate(
-            [jnp.concatenate([one[i] for one in split], axis=1) for i in range(3)], axis=0
+            [jnp.concatenate([one[i] for one in split], axis=1) for i in range(2)], axis=0
         )
         product = lax.dot_general(
             hot[:, low * WALL:high * WALL], scaled, (((1,), (1,)), ((), ())), preferred_element_type=F32
         )
         summed = product if summed is None else summed + product
-    summed = summed[:, 0:ANG] + summed[:, ANG:2 * ANG] + summed[:, 2 * ANG:3 * ANG]
+    summed = sum(summed[:, i * ANG:(i + 1) * ANG] for i in range(1, 2)) + summed[:, 0:ANG]
     packed = jnp.concatenate([summed[0:WIDTH // 2], summed[WIDTH // 2:WIDTH]], axis=1)
     dense[...] = packed.reshape(NB, OWN // 2, 2 * ANG)
 
@@ -534,18 +537,13 @@
         out_shape=tuple(jax.ShapeDtypeStruct(o.shape, o.dtype) for o in outs),
         in_specs=[anyspace] * 3,
         out_specs=(anyspace,) * 3,
-        scratch_shapes=[pltpu.SemaphoreType.DMA((9,))],
+        scratch_shapes=[pltpu.SemaphoreType.DMA((3,))],
         compiler_params=pltpu.CompilerParams(vmem_limit_bytes=1024 * 1024),
     )(*outs)
 
 
 def hand_over(adj_p, adj_v, grad, adj_p_out, adj_v_out, grad_out, sem):
-    pairs = [(grad, grad_out)]
-    for x in range(0, CX, 2):
-        here = pl.ds(x, 2)
-        pairs.append((adj_p.at[here], adj_p_out.at[here]))
-        for k in range(3):
-            pairs.append((adj_v.at[k, here], adj_v_out.at[k, here]))
+    pairs = ((adj_v, adj_v_out), (adj_p, adj_p_out), (grad, grad_out))
     copies = [pltpu.make_async_copy(a, b, sem.at[i]) for i, (a, b) in enumerate(pairs)]
     for copy in copies:
         copy.start()

time: 32.1 us -> 31.6 us (0.984)
  Pallas kernels: 30.1 us -> 29.6 us
    pallas_call x1, Pallas kernels: 29 us -> 28.6 us  [local(): pl.pallas_call(functools.partial(kernel, ns, nr, nc), out_shape=(pltpu.VM...]
where the time goes in v8:
time: 31.6 us; the launch traced here: 31.5 us
  Pallas kernels  29.6 us (94%)
  between operations  1.93 us (6%)
    pallas_call x1, Pallas kernels, local(): pl.pallas_call(functools.partial(kernel, ns, nr, nc), out_shape=(pltpu.VM...  28.6 us
    pallas_call x1, Pallas kernels, written(): pl.pallas_call(hand_over, out_shape=tuple((jax.ShapeDtypeStruct(o.shape,...  0.99 us

profile of v8, /device:TPU:1, one launch (start us, length us, event | category | flops | bytes accessed | tf_op | source)
XLA Modules:
  0.0 31.5 jit_solution(2659704108230352188)
XLA Ops:
  1.9 28.6 %shard_map.139 = (f32[4,128,128]{2,1,0:T(8,128)S(1)}, f32[3,4,128,128]{3,2,1,0:T(8,128)S(1)}, f32[8,64]{1,0:T(8,128)S(1)}) custom-call(f32[4,128,128]{2,1,0:T(8,128)} %p_in.1, f32[3,4,128,128]{3,2,1,0:T(8,128)} %v_in.1, f32[4,128,128]{2,1,0:T(8,128)} %kap_in.1, f32[4,128,128]{2,1,0:T(8,128)} %drv_in.1, f32[4,128,128]{2,1,0:T(8,128)} %ap_in.1, ...), custom_call_target="tpu_custom_call" | custom-call | flops 1000000000 | bytes 4000000 | tf_op jit(solution)/shard_map/pallas_call | solution.py:559
  30.5 1.0 %shard_map.140 = (f32[4,128,128]{2,1,0:T(8,128)}, f32[3,4,128,128]{3,2,1,0:T(8,128)}, f32[8,64]{1,0:T(8,128)}) custom-call(f32[4,128,128]{2,1,0:T(8,128)S(1)} %get-tuple-element.6.adj_p, f32[3,4,128,128]{3,2,1,0:T(8,128)S(1)} %get-tuple-element.7.adj_v, f32[8,64]{1,0:T(8,128)S(1)} %get-tuple-element.8.grad), custom_call_target="tpu_custom_call" | custom-call | tf_op jit(solution)/shard_map/pallas_call | solution.py:535

commit v9 on v8

--- a/solution.py
+++ b/solution.py
@@ -20,13 +20,23 @@
 NA = NXC * NYC
 NB = 2 * ZL * ZH
 WIDTH = NB * OWN
-BATCHES = (0, 5, 11, 16)
 LINE = sorted(range(1, 16), key=lambda k: (-(k & 1), abs((k >> 2) - 2), k))
 MESH = pl.DeviceIdType.MESH
+
+
+def hops(dy, dx):
+    dy, dx = dy % NYC, dx % NXC
+    return min(dy, NYC - dy) + min(dx, NXC - dx)
+
+
 PLANE = sorted(
     ((dy, dx) for dy in range(NYC) for dx in range(NXC)),
-    key=lambda d: (min(d[0], NYC - d[0]) + min(d[1], NXC - d[1]), d),
+    key=lambda d: (d != (0, 0), max(hops(d[0], d[1] + i) for i in (-1, 0, 1)), hops(*d), d),
 )
+BESIDE = [
+    tuple(PLANE.index((dy, (dx + i) % NXC)) for i in (1, -1)) for dy, dx in PLANE
+]
+BATCHES = (0, 6, 13, 16)
 F32 = jnp.float32
 BF16 = jnp.bfloat16
 
@@ -46,13 +56,13 @@
     cells_ref, rows_ref, angle_ref, count_ref, step_ref,
     pp, qq, kap, drv, ap, vel, total, mask,
     lam0, lam1, lam2, apo, q_near,
-    zsend, zrecv, lsend, lrecv,
+    zsend, zrecv, lsend, lrecv, z_far, l_far, asking, asked,
     turned_face, turned_wrap, face_parts, wrap_parts, slot_parts,
     cells_buf, answer, answered,
     ends, own_hot_y,
     slots, vals, hot, weight, where_hot, sens_t, dense, parts,
     small_sem, load_sem, store_sem, halo_send, halo_recv, lam_send, lam_recv,
-    wrap_send, wrap_recv, cell_send, cell_recv, answer_send, answer_recv,
+    info_send, info_recv, wrap_send, wrap_recv, cell_send, cell_recv, answer_send, answer_recv,
     slot_send, slot_recv, val_send, val_recv, part_send, part_recv,
 ):
     s = lax.axis_index("slab")
@@ -85,8 +95,9 @@
         ref[1] = plane
     lam0[0] = plane
     lam0[CX + 1] = plane
-    zrecv[...] = jnp.zeros_like(zrecv)
-    lrecv[...] = jnp.zeros_like(lrecv)
+    z_far[...] = jnp.zeros_like(z_far)
+    l_far[...] = jnp.zeros_like(l_far)
+    asked[...] = jnp.zeros_like(asked)
     answered[...] = jnp.zeros_like(answered)
 
     barrier = pltpu.get_barrier_semaphore()
@@ -96,17 +107,20 @@
 
     s_up, s_down = jnp.minimum(s + 1, ns - 1), jnp.maximum(s - 1, 0)
     r_up, r_down = jnp.minimum(r + 1, nr - 1), jnp.maximum(r - 1, 0)
-    c_up, c_down = jnp.minimum(c + 1, nc - 1), jnp.maximum(c - 1, 0)
     has = {
-        "xu": s < ns - 1, "xd": s > 0, "yu": r < nr - 1, "yd": r > 0, "zu": c < nc - 1, "zd": c > 0,
+        "xu": s < ns - 1, "xd": s > 0, "yu": r < nr - 1, "yd": r > 0,
     }
     wrap_up = jnp.logical_and(zl == ZL - 1, has["xu"])
     wrap_down = jnp.logical_and(zl == 0, has["xd"])
+    c_pair = c ^ 1
+    aside = 1 - 2 * zh
+    has_served = jnp.logical_and(x_at + aside >= 0, x_at + aside < NXC)
+    has_server = jnp.logical_and(x_at - aside >= 0, x_at - aside < NXC)
+    c_served = jnp.clip(x_at + aside, 0, NXC - 1) * ZH + zh
+    c_server = jnp.clip(x_at - aside, 0, NXC - 1) * ZH + zh
     near_up = zl < ZL - 1
     near_down = zl > 0
     beyond = (
-        (jnp.logical_and(zh == ZH - 1, has["zu"]), (s, r, c_up)),
-        (jnp.logical_and(zh == 0, has["zd"]), (s, r, c_down)),
         (wrap_up, (s_up, r, c)),
         (wrap_down, (s_down, r, c)),
     )
@@ -248,10 +262,20 @@
         "xu": halo(answer.at[1], answered.at[0], 0, answer_send, answer_recv, (s_up, r, c)),
         "xd": halo(answer.at[0], answered.at[1], 1, answer_send, answer_recv, (s_down, r, c)),
     }
-    pq_z = {
-        "zu": halo(zsend.at[pl.ds(8, 8)], zrecv.at[pl.ds(0, 8)], 8, halo_send, halo_recv, (s, r, c_up)),
-        "zd": halo(zsend.at[pl.ds(0, 8)], zrecv.at[pl.ds(8, 8)], 9, halo_send, halo_recv, (s, r, c_down)),
-    }
+    pq_z = halo(zsend, zrecv, 8, halo_send, halo_recv, (s, r, c_pair))
+    lam_z = halo(lsend, lrecv, 4, lam_send, lam_recv, (s, r, c_pair))
+    info = halo(asking, asked, 0, info_send, info_recv, (s, r, c_server))
+
+    def onward(src, dst, at):
+        return [halo(src.at[pl.ds(8 * (1 - h), 8)], dst, at, info_send, info_recv, (s, r, c_served)) for h in range(ZH)]
+
+    z_on = onward(zrecv, z_far, 1)
+    l_on = onward(lrecv, l_far, 2)
+
+    def start_on(copies):
+        for h in range(ZH):
+            pl.when(jnp.logical_and(has_served, zh == h))(copies[h].start)
+
     lam_x = {
         "xu": halo(lam0.at[CX], lam0.at[0], 0, lam_send, lam_recv, (s_up, r, c)),
         "xd": halo(lam0.at[1], lam0.at[CX + 1], 1, lam_send, lam_recv, (s_down, r, c)),
@@ -260,16 +284,12 @@
         "yu": halo(lam1.at[inner, pl.ds(CY, 8)], lam1.at[inner, pl.ds(0, 8)], 2, lam_send, lam_recv, (s, r_up, c)),
         "yd": halo(lam1.at[inner, pl.ds(8, 8)], lam1.at[inner, pl.ds(CY + 8, 8)], 3, lam_send, lam_recv, (s, r_down, c)),
     }
-    lam_z = {
-        "zu": halo(lsend.at[pl.ds(8, 8)], lrecv.at[pl.ds(0, 8)], 4, lam_send, lam_recv, (s, r, c_up)),
-        "zd": halo(lsend.at[pl.ds(0, 8)], lrecv.at[pl.ds(8, 8)], 5, lam_send, lam_recv, (s, r, c_down)),
-    }
 
     def start(faces):
         for side, copy in faces.items():
             pl.when(has[side])(copy.start)
 
-    opposite = {"xu": "xd", "xd": "xu", "yu": "yd", "yd": "yu", "zu": "zd", "zd": "zu"}
+    opposite = {"xu": "xd", "xd": "xu", "yu": "yd", "yd": "yu"}
 
     def arrive(faces):
         for side, copy in faces.items():
@@ -279,7 +299,7 @@
         for side, copy in faces.items():
             pl.when(has[side])(copy.wait_send)
 
-    start(pq_z)
+    pq_z.start()
     start(q_y)
     start(p_y)
     pl.when(near_up)(ask["xu"].start)
@@ -300,6 +320,32 @@
     phase = jnp.cos(0.5 * jnp.full((1, CZ), lax.rem(step_ref[0], 97).astype(F32), F32))
     for copy in loads[3:]:
         copy.wait()
+    at_z = lax.broadcasted_iota(jnp.int32, (CY, CZ), 1)
+
+    def along_z(field):
+        upper = jnp.where(at_z == CZ - 1, 0.0, pltpu.roll(field, CZ - 1, 1))
+        lower = jnp.where(at_z == 0, 0.0, pltpu.roll(field, 1, 1))
+        return (upper - lower) * 0.5
+
+    for x in range(CX):
+        here = slice(x * CY, (x + 1) * CY)
+        total_2 = total[2, x] + along_z(qq[x, rows_of])
+        moved_2 = vel[2, x] - 0.3 * along_z(pp[x, rows_of])
+        total[2, x] = total_2
+        apo[x] = total_2 * moved_2
+        for i, field in enumerate((total_2.T, moved_2.T)):
+            ends[i:i + 1, here] = field[0:1]
+            ends[2 + i:3 + i, here] = field[CZ - 1:CZ]
+    edge_parts = jnp.concatenate(pieces(ends[...]), axis=0)
+    edge = jnp.dot(edge_parts, where_hot[...], preferred_element_type=F32)
+    edge = edge[0:4] + edge[4:8] + edge[8:12]
+    far_edge = jnp.where(zh == 0, edge[0:2], edge[2:4])
+    near_edge = jnp.where(zh == 0, edge[2:4], edge[0:2])
+    asking[0:2] = far_edge
+    asking[2:3] = own_cells.astype(F32)
+    asking[3:4] = own_cells.astype(F32)
+    pl.when(has_server)(info.start)
+
     arrive(q_y)
     arrive(p_y)
 
@@ -313,33 +359,18 @@
     def along_y(ref, x):
         return (ref[x, pl.ds(9, CY)] - ref[x, pl.ds(7, CY)]) * 0.5
 
-    at_z = lax.broadcasted_iota(jnp.int32, (CY, CZ), 1)
-
-    def along_z(field):
-        upper = jnp.where(at_z == CZ - 1, 0.0, pltpu.roll(field, CZ - 1, 1))
-        lower = jnp.where(at_z == 0, 0.0, pltpu.roll(field, 1, 1))
-        return (upper - lower) * 0.5
-
     for x in range(CX):
         here = slice(x * CY, (x + 1) * CY)
         total_0 = total[0, x] + along_x(qq, x)
         total_1 = total[1, x] + along_y(qq, x)
-        total_2 = total[2, x] + along_z(qq[x, rows_of])
         total[0, x] = total_0
         total[1, x] = total_1
-        total[2, x] = total_2
         moved_0 = vel[0, x] - 0.3 * along_x(pp, x) + drv[x] * phase
-        moved_2 = vel[2, x] - 0.3 * along_z(pp[x, rows_of])
-        sens = -(
-            total_0 * moved_0 + total_1 * (vel[1, x] - 0.3 * along_y(pp, x)) + total_2 * moved_2
-        )
+        sens = -(total_0 * moved_0 + total_1 * (vel[1, x] - 0.3 * along_y(pp, x)) + apo[x])
         for i, piece in enumerate(pieces(sens.T)):
             sens_t[i * CZ:(i + 1) * CZ, here] = piece
         if x in (0, CX - 1):
             split_into(slot_parts.at[x // (CX - 1)], total_0.T, moved_0.T)
-        for i, field in enumerate((total_2.T, moved_2.T)):
-            ends[i:i + 1, here] = field[0:1]
-            ends[2 + i:3 + i, here] = field[CZ - 1:CZ]
 
     def serve(side, at):
         cells = cells_buf[at]
@@ -367,31 +398,39 @@
         for side in range(2)
     ]
 
-    edge_parts = jnp.concatenate(pieces(ends[...]), axis=0)
-    edge = jnp.dot(edge_parts, where_hot[...], preferred_element_type=F32)
-    edge = edge[0:4] + edge[4:8] + edge[8:12]
-
     picked = jnp.dot(sens_t[...], where_hot[...], preferred_element_type=F32)
     picked = picked[0:CZ] + picked[CZ:2 * CZ] + picked[2 * CZ:3 * CZ]
     picked = jnp.sum(jnp.where(y_at == own_z, picked, 0.0), axis=0, keepdims=True)
 
-    def corrected(value, side, here, total_at, moved_at, p_at, q_at):
-        sign = 2.0 * side - 1.0
+    def correction(sign, here, total_at, moved_at, p_at, q_at):
         more_total = jnp.where(here, q_at, 0.0) * (0.5 * sign)
         more_moved = jnp.where(here, p_at, 0.0) * (-0.15 * sign)
-        return value - (more_total * (moved_at + more_moved) + total_at * more_moved)
-
-    arrive(pq_z)
-    z_parts = jnp.concatenate(pieces(zrecv[...]), axis=0)
-    faces_z = jnp.dot(z_parts, own_hot_y[...], preferred_element_type=F32)
-    faces_z = faces_z[0:16] + faces_z[16:32] + faces_z[32:48]
-    row_x = lax.broadcasted_iota(jnp.int32, (16, WALL), 0) & (CX - 1)
-    faces_z = jnp.where(row_x == own_x, faces_z, 0.0)
-    for side in range(2):
-        p_at = jnp.sum(faces_z[8 * side:8 * side + 4], axis=0, keepdims=True)
-        q_at = jnp.sum(faces_z[8 * side + 4:8 * side + 8], axis=0, keepdims=True)
-        here = own_z == side * (CZ - 1)
-        picked = corrected(picked, side, here, edge[2 * side:2 * side + 1], edge[2 * side + 1:2 * side + 2], p_at, q_at)
+        return -(more_total * (moved_at + more_moved) + total_at * more_moved)
+
+    row_x = lax.broadcasted_iota(jnp.int32, (8, WALL), 0) & (CX - 1)
+
+    def face_at(rows, hot_y, at_x):
+        got = jnp.dot(jnp.concatenate(pieces(rows), axis=0), hot_y, preferred_element_type=F32)
+        got = jnp.where(row_x == at_x, got[0:8] + got[8:16] + got[16:24], 0.0)
+        return jnp.sum(got[0:4], axis=0, keepdims=True), jnp.sum(got[4:8], axis=0, keepdims=True)
+
+    pl.when(has_served)(info.wait_recv)
+    served_cells = asked[2:3].astype(jnp.int32)
+    served_hot = hot_y_of(served_cells)
+    pq_z.wait_recv()
+    start_on(z_on)
+    near_face = jnp.where(zh == 0, zrecv[0:8], zrecv[8:16])
+    far_face = jnp.where(zh == 0, zrecv[8:16], zrecv[0:8])
+    sign = aside.astype(F32)
+    near_end = (CZ - 1) * (1 - zh)
+    far_end = (CZ - 1) * zh
+    p_at, q_at = face_at(near_face, own_hot_y[...], own_x)
+    picked = picked + correction(sign, own_z == near_end, near_edge[0:1], near_edge[1:2], p_at, q_at)
+    p_at, q_at = face_at(far_face, served_hot, served_cells >> 14)
+    on_edge = jnp.logical_and((served_cells & (CZ - 1)) == far_end, has_served)
+    vals[0, 1:2] = jnp.where(
+        on_edge, correction(-sign, on_edge, asked[0:1], asked[1:2], p_at, q_at), 0.0
+    )
 
     pl.when(near_down)(reply["xu"].wait_recv)
     pl.when(near_up)(reply["xd"].wait_recv)
@@ -414,8 +453,8 @@
 
     for side, (total_at, moved_at) in enumerate(on_face):
         here = own_x == side * (CX - 1)
-        picked = corrected(picked, side, here, total_at, moved_at, answered[side, 0:1], answered[side, 1:2])
-    vals[0] = picked
+        picked = picked + correction(2.0 * side - 1.0, here, total_at, moved_at, answered[side, 0:1], answered[side, 1:2])
+    vals[0, 0:1] = picked
 
     for k in range(NA - 1, 0, -1):
         pltpu.make_async_remote_copy(
@@ -434,7 +473,13 @@
     def _():
         q_near[1] = turned_wrap[1].T
 
-    edge_t = jnp.concatenate([zrecv[...], jnp.zeros((CZ - 16, CZ), F32)], axis=0).T
+    def both_edges(pair, far):
+        lower = jnp.where(zh == 0, far[...], pair[8:16])
+        upper = jnp.where(zh == 0, pair[0:8], far[...])
+        return jnp.concatenate([lower, upper, jnp.zeros((CZ - 16, CZ), F32)], axis=0).T
+
+    pl.when(has_server)(z_on[0].wait_recv)
+    edge_t = both_edges(zrecv, z_far)
 
     def with_edges(field, low, high):
         field = jnp.where(at_z == CZ - 1, field + high * 0.5, field)
@@ -458,7 +503,7 @@
         turned = lam2[x].T
         lsend[x:x + 1] = turned[0:1]
         lsend[8 + x:9 + x] = turned[CZ - 1:CZ]
-    start(lam_z)
+    lam_z.start()
     stores = [
         pltpu.make_async_copy(lam0.at[pl.ds(1, CX)], av_out.at[0], store_sem.at[0]),
         pltpu.make_async_copy(lam1.at[pl.ds(0, CX), rows_of], av_out.at[1], store_sem.at[1]),
@@ -477,10 +522,16 @@
 
     rest_vals = vals.at[pl.ds(1, NA - 1)]
     summed = None
+    seen = {0}
     for low, high in zip(BATCHES[:-1], BATCHES[1:]):
-        for k in range(max(low, 1), high):
+        for k in sorted({k for j in range(low, high) for k in (j,) + BESIDE[j]} - seen):
             pltpu.make_async_copy(vals.at[k], vals.at[k], val_recv.at[k]).wait()
-        split = [pieces(weight[k] * vals[k])[:2] for k in range(low, high)]
+            seen.add(k)
+        value = [
+            vals[k, 0:1] + jnp.where(zh == 0, vals[BESIDE[k][0], 1:2], vals[BESIDE[k][1], 1:2])
+            for k in range(low, high)
+        ]
+        split = [pieces(weight[k] * value[k - low])[:2] for k in range(low, high)]
         scaled = jnp.concatenate(
             [jnp.concatenate([one[i] for one in split], axis=1) for i in range(2)], axis=0
         )
@@ -499,9 +550,12 @@
             send_sem=part_send, recv_sem=part_recv, device_id=line_peer(k), device_id_type=MESH,
         ).start()
 
-    for faces in (lam_x, lam_y, lam_z):
-        arrive(faces)
-    edge_l = jnp.concatenate([lrecv[...], jnp.zeros((CZ - 16, CZ), F32)], axis=0).T
+    lam_z.wait_recv()
+    start_on(l_on)
+    arrive(lam_x)
+    arrive(lam_y)
+    pl.when(has_server)(l_on[0].wait_recv)
+    edge_l = both_edges(lrecv, l_far)
     for x in range(CX):
         div = (
             (lam0[x + 2] - lam0[x]) * 0.5
@@ -516,8 +570,13 @@
     own = dense[b] + jnp.sum(parts[...], axis=0)
     grad_out[...] = jnp.concatenate([own[:, 0:ANG], own[:, ANG:2 * ANG]], axis=0)
 
-    for faces in (q_y, p_y, pq_z, lam_x, lam_y, lam_z):
+    for faces in (q_y, p_y, lam_x, lam_y):
         sent(faces)
+    pq_z.wait_send()
+    lam_z.wait_send()
+    pl.when(has_server)(info.wait_send)
+    pl.when(has_served)(z_on[0].wait_send)
+    pl.when(has_served)(l_on[0].wait_send)
     pl.when(wrap_up)(wrap["xu"].wait_send)
     pl.when(wrap_down)(wrap["xd"].wait_send)
     for faces in (ask, reply, q_x):
@@ -588,6 +647,10 @@
             pltpu.VMEM((16, CY), F32),
             pltpu.VMEM((16, CY), F32),
             pltpu.VMEM((16, CY), F32),
+            pltpu.VMEM((8, CY), F32),
+            pltpu.VMEM((8, CY), F32),
+            pltpu.VMEM((4, WALL), F32),
+            pltpu.VMEM((4, WALL), F32),
             pltpu.VMEM((2, 2, CZ, CY), F32),
             pltpu.VMEM((2, CZ, CY), F32),
             pltpu.VMEM((2, 6 * CZ, CY), BF16),
@@ -599,14 +662,14 @@
             pltpu.VMEM((4, CX * CY), F32),
             pltpu.VMEM((CY, WALL), BF16),
             pltpu.VMEM((NA, 2, WALL), F32),
-            pltpu.VMEM((NA, 1, WALL), F32),
+            pltpu.VMEM((NA, 2, WALL), F32),
             pltpu.VMEM((WIDTH, NA * WALL), BF16),
             pltpu.VMEM((NA, ANG, WALL), F32),
             pltpu.VMEM((CX * CY, WALL), BF16),
             pltpu.VMEM((3 * CZ, CX * CY), BF16),
             pltpu.VMEM((NB, OWN // 2, 2 * ANG), F32),
             pltpu.VMEM((NB - 1, OWN // 2, 2 * ANG), F32),
-            dma((5,)), dma((7,)), dma((4,)), dma((10,)), dma((10,)), dma((6,)), dma((6,)),
+            dma((5,)), dma((7,)), dma((4,)), dma((10,)), dma((10,)), dma((6,)), dma((6,)), dma((3,)), dma((3,)),
             dma((2,)), dma((2,)), dma((2,)), dma((2,)), dma((2,)), dma((2,)),
             dma, dma((NA,)), dma, dma((NA,)), dma, dma,
         ],

time: 31.6 us -> 32 us (1.013)
  Pallas kernels: 29.6 us -> 30 us
    pallas_call x1, Pallas kernels: 28.6 us -> 29 us  [local(): pl.pallas_call(functools.partial(kernel, ns, nr, nc), out_shape=(pltpu.VM...]
where the time goes in v9:
time: 32 us; the launch traced here: 31.9 us
  Pallas kernels  30 us (94%)
  between operations  1.93 us (6%)
    pallas_call x1, Pallas kernels, local(): pl.pallas_call(functools.partial(kernel, ns, nr, nc), out_shape=(pltpu.VM...  29 us
    pallas_call x1, Pallas kernels, written(): pl.pallas_call(hand_over, out_shape=tuple((jax.ShapeDtypeStruct(o.shape,...  0.99 us

profile of v9, /device:TPU:1, one launch (start us, length us, event | category | flops | bytes accessed | tf_op | source)
XLA Modules:
  0.0 31.9 jit_solution(17751599090028951216)
XLA Ops:
  1.9 29.0 %shard_map.139 = (f32[4,128,128]{2,1,0:T(8,128)S(1)}, f32[3,4,128,128]{3,2,1,0:T(8,128)S(1)}, f32[8,64]{1,0:T(8,128)S(1)}) custom-call(f32[4,128,128]{2,1,0:T(8,128)} %p_in.1, f32[3,4,128,128]{3,2,1,0:T(8,128)} %v_in.1, f32[4,128,128]{2,1,0:T(8,128)} %kap_in.1, f32[4,128,128]{2,1,0:T(8,128)} %drv_in.1, f32[4,128,128]{2,1,0:T(8,128)} %ap_in.1, ...), custom_call_target="tpu_custom_call" | custom-call | flops 1000000000 | bytes 4000000 | tf_op jit(solution)/shard_map/pallas_call | solution.py:618
  30.9 1.0 %shard_map.140 = (f32[4,128,128]{2,1,0:T(8,128)}, f32[3,4,128,128]{3,2,1,0:T(8,128)}, f32[8,64]{1,0:T(8,128)}) custom-call(f32[4,128,128]{2,1,0:T(8,128)S(1)} %get-tuple-element.6.adj_p, f32[3,4,128,128]{3,2,1,0:T(8,128)S(1)} %get-tuple-element.7.adj_v, f32[8,64]{1,0:T(8,128)S(1)} %get-tuple-element.8.grad), custom_call_target="tpu_custom_call" | custom-call | tf_op jit(solution)/shard_map/pallas_call | solution.py:594

commit v10 on v8

--- a/solution.py
+++ b/solution.py
@@ -381,6 +381,29 @@
         more_moved = jnp.where(here, p_at, 0.0) * (-0.15 * sign)
         return value - (more_total * (moved_at + more_moved) + total_at * more_moved)
 
+    pl.when(near_down)(reply["xu"].wait_recv)
+    pl.when(near_up)(reply["xd"].wait_recv)
+
+    def own_answer(side):
+        split_into(wrap_parts, turned_wrap[0], turned_wrap[1])
+        p_at, q_at = pick(wrap_parts, own_hot_y[...], cells_buf[0] & (CZ - 1))
+        answered[side, 0:1] = p_at
+        answered[side, 1:2] = q_at
+
+    @pl.when(wrap_down)
+    def _():
+        wrap["xu"].wait_recv()
+        own_answer(0)
+
+    @pl.when(wrap_up)
+    def _():
+        wrap["xd"].wait_recv()
+        own_answer(1)
+
+    for side, (total_at, moved_at) in enumerate(on_face):
+        here = own_x == side * (CX - 1)
+        picked = corrected(picked, side, here, total_at, moved_at, answered[side, 0:1], answered[side, 1:2])
+
     arrive(pq_z)
     z_parts = jnp.concatenate(pieces(zrecv[...]), axis=0)
     faces_z = jnp.dot(z_parts, own_hot_y[...], preferred_element_type=F32)
@@ -392,29 +415,6 @@
         q_at = jnp.sum(faces_z[8 * side + 4:8 * side + 8], axis=0, keepdims=True)
         here = own_z == side * (CZ - 1)
         picked = corrected(picked, side, here, edge[2 * side:2 * side + 1], edge[2 * side + 1:2 * side + 2], p_at, q_at)
-
-    pl.when(near_down)(reply["xu"].wait_recv)
-    pl.when(near_up)(reply["xd"].wait_recv)
-
-    def own_answer(side):
-        split_into(wrap_parts, turned_wrap[0], turned_wrap[1])
-        p_at, q_at = pick(wrap_parts, own_hot_y[...], cells_buf[0] & (CZ - 1))
-        answered[side, 0:1] = p_at
-        answered[side, 1:2] = q_at
-
-    @pl.when(wrap_down)
-    def _():
-        wrap["xu"].wait_recv()
-        own_answer(0)
-
-    @pl.when(wrap_up)
-    def _():
-        wrap["xd"].wait_recv()
-        own_answer(1)
-
-    for side, (total_at, moved_at) in enumerate(on_face):
-        here = own_x == side * (CX - 1)
-        picked = corrected(picked, side, here, total_at, moved_at, answered[side, 0:1], answered[side, 1:2])
     vals[0] = picked
 
     for k in range(NA - 1, 0, -1):

time: 31.6 us -> 31.8 us (level)
  no operation moved by 1% of the time
where the time goes in v10:
time: 31.8 us; the launch traced here: 31.7 us
  Pallas kernels  29.8 us (94%)
  between operations  1.93 us (6%)
    pallas_call x1, Pallas kernels, local(): pl.pallas_call(functools.partial(kernel, ns, nr, nc), out_shape=(pltpu.VM...  28.8 us
    pallas_call x1, Pallas kernels, written(): pl.pallas_call(hand_over, out_shape=tuple((jax.ShapeDtypeStruct(o.shape,...  0.99 us

profile of v10, /device:TPU:1, one launch (start us, length us, event | category | flops | bytes accessed | tf_op | source)
XLA Modules:
  0.0 31.7 jit_solution(8481973004629659306)
XLA Ops:
  1.9 28.8 %shard_map.139 = (f32[4,128,128]{2,1,0:T(8,128)S(1)}, f32[3,4,128,128]{3,2,1,0:T(8,128)S(1)}, f32[8,64]{1,0:T(8,128)S(1)}) custom-call(f32[4,128,128]{2,1,0:T(8,128)} %p_in.1, f32[3,4,128,128]{3,2,1,0:T(8,128)} %v_in.1, f32[4,128,128]{2,1,0:T(8,128)} %kap_in.1, f32[4,128,128]{2,1,0:T(8,128)} %drv_in.1, f32[4,128,128]{2,1,0:T(8,128)} %ap_in.1, ...), custom_call_target="tpu_custom_call" | custom-call | flops 1000000000 | bytes 4000000 | tf_op jit(solution)/shard_map/pallas_call | solution.py:559
  30.7 1.0 %shard_map.140 = (f32[4,128,128]{2,1,0:T(8,128)}, f32[3,4,128,128]{3,2,1,0:T(8,128)}, f32[8,64]{1,0:T(8,128)}) custom-call(f32[4,128,128]{2,1,0:T(8,128)S(1)} %get-tuple-element.6.adj_p, f32[3,4,128,128]{3,2,1,0:T(8,128)S(1)} %get-tuple-element.7.adj_v, f32[8,64]{1,0:T(8,128)S(1)} %get-tuple-element.8.grad), custom_call_target="tpu_custom_call" | custom-call | tf_op jit(solution)/shard_map/pallas_call | solution.py:535

commit v11 on v10

--- a/solution.py
+++ b/solution.py
@@ -192,6 +192,8 @@
             for j, piece in enumerate(pieces(field)[:picks]):
                 ref[(picks * i + j) * CZ:(picks * i + j + 1) * CZ] = piece
 
+    y_at = lax.broadcasted_iota(jnp.int32, (CY, WALL), 0)
+
     def pick(ref, hot_y, at_z):
         got = jnp.dot(ref[0:2 * picks * CZ], hot_y, preferred_element_type=F32)
         out = []
@@ -206,6 +208,13 @@
         return jnp.where(y_at == ((cells >> 7) & (CY - 1)), 1.0, 0.0).astype(BF16)
 
 
+    for x in range(CX):
+        where_hot[x * CY:(x + 1) * CY] = jnp.where(y_at + x * CY == own_xy, 1.0, 0.0).astype(BF16)
+    own_hot_y[...] = hot_y_of(own_cells)
+    for side in range(2):
+        split_into(face_parts.at[side], turned_face[side, 0], turned_face[side, 1])
+    prepare(0)
+
     pl.semaphore_wait(barrier, partners)
 
     def slot_copy(k):
@@ -289,13 +298,6 @@
     for k in range(NA - 1, 0, -1):
         slot_copy(k).start()
 
-    y_at = lax.broadcasted_iota(jnp.int32, (CY, WALL), 0)
-    for x in range(CX):
-        where_hot[x * CY:(x + 1) * CY] = jnp.where(y_at + x * CY == own_xy, 1.0, 0.0).astype(BF16)
-    own_hot_y[...] = hot_y_of(own_cells)
-    for side in range(2):
-        split_into(face_parts.at[side], turned_face[side, 0], turned_face[side, 1])
-    prepare(0)
 
     phase = jnp.cos(0.5 * jnp.full((1, CZ), lax.rem(step_ref[0], 97).astype(F32), F32))
     for copy in loads[3:]:
@@ -371,6 +373,13 @@
     edge = jnp.dot(edge_parts, where_hot[...], preferred_element_type=F32)
     edge = edge[0:4] + edge[4:8] + edge[8:12]
 
+    def slots_of(k, _):
+        pltpu.make_async_copy(slots.at[k], slots.at[k], slot_recv.at[k]).wait()
+        prepare(k)
+        return 0
+
+    lax.fori_loop(1, BATCHES[1], slots_of, 0)
+
     picked = jnp.dot(sens_t[...], where_hot[...], preferred_element_type=F32)
     picked = picked[0:CZ] + picked[CZ:2 * CZ] + picked[2 * CZ:3 * CZ]
     picked = jnp.sum(jnp.where(y_at == own_z, picked, 0.0), axis=0, keepdims=True)
@@ -467,13 +476,8 @@
     for copy in stores:
         copy.start()
 
-    def slots_of(k, _):
-        pltpu.make_async_copy(slots.at[k], slots.at[k], slot_recv.at[k]).wait()
-        prepare(k)
-        return 0
-
     rest = slots.at[pl.ds(1, NA - 1)]
-    lax.fori_loop(1, NA, slots_of, 0)
+    lax.fori_loop(BATCHES[1], NA, slots_of, 0)
 
     rest_vals = vals.at[pl.ds(1, NA - 1)]
     summed = None

time: 31.8 us -> 31.8 us (level)
  no operation moved by 1% of the time
where the time goes in v11:
time: 31.8 us; the launch traced here: 31.7 us
  Pallas kernels  29.8 us (94%)
  between operations  1.93 us (6%)
    pallas_call x1, Pallas kernels, local(): pl.pallas_call(functools.partial(kernel, ns, nr, nc), out_shape=(pltpu.VM...  28.8 us
    pallas_call x1, Pallas kernels, written(): pl.pallas_call(hand_over, out_shape=tuple((jax.ShapeDtypeStruct(o.shape,...  0.99 us

profile of v11, /device:TPU:1, one launch (start us, length us, event | category | flops | bytes accessed | tf_op | source)
XLA Modules:
  0.0 31.7 jit_solution(6906716962888841622)
XLA Ops:
  1.9 28.8 %shard_map.139 = (f32[4,128,128]{2,1,0:T(8,128)S(1)}, f32[3,4,128,128]{3,2,1,0:T(8,128)S(1)}, f32[8,64]{1,0:T(8,128)S(1)}) custom-call(f32[4,128,128]{2,1,0:T(8,128)} %p_in.1, f32[3,4,128,128]{3,2,1,0:T(8,128)} %v_in.1, f32[4,128,128]{2,1,0:T(8,128)} %kap_in.1, f32[4,128,128]{2,1,0:T(8,128)} %drv_in.1, f32[4,128,128]{2,1,0:T(8,128)} %ap_in.1, ...), custom_call_target="tpu_custom_call" | custom-call | flops 1000000000 | bytes 4000000 | tf_op jit(solution)/shard_map/pallas_call | solution.py:563
  30.7 1.0 %shard_map.140 = (f32[4,128,128]{2,1,0:T(8,128)}, f32[3,4,128,128]{3,2,1,0:T(8,128)}, f32[8,64]{1,0:T(8,128)}) custom-call(f32[4,128,128]{2,1,0:T(8,128)S(1)} %get-tuple-element.6.adj_p, f32[3,4,128,128]{3,2,1,0:T(8,128)S(1)} %get-tuple-element.7.adj_v, f32[8,64]{1,0:T(8,128)S(1)} %get-tuple-element.8.grad), custom_call_target="tpu_custom_call" | custom-call | tf_op jit(solution)/shard_map/pallas_call | solution.py:539
